TPU v7x, 128 devices: a whole 4x4x4 slice. The times are simulated.
128 devices in a mesh: section: 16 (over z_hi, y, core), tp: 8 (over z_lo, x).
Axes of the slice: x: 4, y: 4, z: 4 (z_hi: 2, z_lo: 2; z = z_hi * 2 + z_lo), core: 2. Of those that a mesh axis runs over, the one named last changes fastest.
Arguments:
- arriving: bfloat16 [16, 256, 6144], P('section', None, 'tp'), may hold values from -6 to 6
- cotangent: bfloat16 [16, 256, 6144], P('section', None, 'tp'), may hold values from -6 to 6
- evicted: bfloat16 [16, 2, 256, 6144], P('section', None, None, 'tp'), may hold values from -6 to 6
- ln_gain: float32 [16, 6144], P('section'), may hold values from 0.25 to 1.75
- value_weight: bfloat16 [16, 6144, 6144], P('section', None, 'tp'), may hold values from -0.076546554 to 2.0765466
- out_weight: bfloat16 [16, 6144, 6144], P('section', 'tp'), may hold values from -0.078125 to 0.078125
- fetch_slot: int32 [16], replicated, may hold values from 0 to 1
Outputs:
- forwarded: bfloat16 [16, 256, 6144], P('section', None, 'tp')
- returned: bfloat16 [16, 256, 6144], P('section', None, 'tp')
- gain_grad: float32 [16, 6144], P('section', 'tp')
- fetched: bfloat16 [16, 256, 6144], P('section', None, 'tp')
All inputs are finite; a program needn't handle non-finite values.
Results may differ from a plain program's by a relative error of at most 0.017.
Values may be sent and summed in bfloat16 or wider, within the bound.
A program may use at most 128 MiB of HBM per device.

v0:
```python
import math

import jax
import jax.numpy as jnp
from jax import lax
from jax.sharding import PartitionSpec as P

HD = 128


EPS = 1e-05


def partner_2(value, axis, apart):
    return lax.ppermute(value, axis, [(i, i ^ 1 << apart) for i in range(lax.axis_size(axis))])


def shifted(block, axis, distance):
    devices = range(lax.axis_size(axis))
    route = [((i - distance) % len(devices), i) for i in devices]
    return lax.ppermute(block, axis, route)


def layer_norm(row_block, gain_row):
    values = row_block.astype(jnp.float32)
    full_width = row_block.shape[1]
    centre = jnp.sum(values, axis=-1, keepdims=True) / full_width
    spread = jnp.sum(values * values, axis=-1, keepdims=True) / full_width - centre * centre
    inv_std = lax.rsqrt(spread + EPS)
    normed = (values - centre) * inv_std
    return (normed, inv_std, (normed * gain_row).astype(jnp.bfloat16))


def head_view(row_block):
    return row_block.reshape(row_block.shape[0], row_block.shape[1] // HD, HD)


def local_attention(queries, values):
    q_heads = head_view(queries)
    v_heads = head_view(values)
    length = queries.shape[0]
    scores = jnp.einsum(
        "qhd,khd->hqk", q_heads, v_heads, preferred_element_type=jnp.float32
    ) / math.sqrt(HD)
    causal = jnp.arange(length)[:, None] >= jnp.arange(length)[None, :]
    scores = jnp.where(causal[None], scores, -jnp.inf)
    attn_probs = jax.nn.softmax(scores, axis=-1)
    probs_low = attn_probs.astype(jnp.bfloat16)
    context = jnp.einsum("hqk,khd->qhd", probs_low, v_heads, preferred_element_type=jnp.float32)
    return (attn_probs, probs_low, context.reshape(length, -1).astype(jnp.bfloat16))


def local_attention_grad(queries, values, attn_probs, probs_low, grad_context):
    q_heads = head_view(queries)
    v_heads = head_view(values)
    g_heads = head_view(grad_context)
    length = queries.shape[0]
    grad_probs = jnp.einsum("qhd,khd->hqk", g_heads, v_heads, preferred_element_type=jnp.float32)
    grad_scores = (
        attn_probs
        * (grad_probs - jnp.sum(grad_probs * attn_probs, axis=-1, keepdims=True))
        / math.sqrt(HD)
    )
    grad_low = grad_scores.astype(jnp.bfloat16)
    grad_values = jnp.einsum("hqk,qhd->khd", probs_low, g_heads, preferred_element_type=jnp.float32)
    grad_values = grad_values + jnp.einsum(
        "hqk,qhd->khd", grad_low, q_heads, preferred_element_type=jnp.float32
    )
    grad_queries = jnp.einsum("hqk,khd->qhd", grad_low, v_heads, preferred_element_type=jnp.float32)
    return (grad_values.reshape(length, -1).astype(jnp.bfloat16), grad_queries.reshape(length, -1))


def body(arriving, cotangent, evicted, ln_gain, value_weight, out_weight, fetch_slot):
    sections = lax.axis_size("section")
    position = lax.axis_index("section")
    tp_rank = lax.axis_index("tp")
    levels = sections.bit_length() - 1
    own_rows = arriving[0]
    own_grad = cotangent[0]
    shard_width = own_rows.shape[1]
    gain_row = ln_gain[0]
    value_local = value_weight[0]
    output_local = out_weight[0]
    head_cols = value_local.shape[1]
    partner = sections - 1 - position
    send_slot = fetch_slot[partner]
    outgoing = lax.dynamic_index_in_dim(evicted[0], send_slot, 0, keepdims=False)
    is_early = position < sections // 2
    shard_start = tp_rank * shard_width
    inputs_full, grad_full, travelling = (
        lax.all_gather(own_rows, "tp", axis=1, tiled=True),
        lax.all_gather(own_grad, "tp", axis=1, tiled=True),
        lax.all_gather(outgoing, "tp", axis=1, tiled=True),
    )
    for bit_index in range(levels):
        travelling = partner_2(travelling, "section", bit_index)
    fetched_share = lax.dynamic_slice_in_dim(travelling, shard_start, shard_width, 1)
    saved_full = jnp.where(is_early, travelling, inputs_full)
    full_width = inputs_full.shape[1]
    col_start = tp_rank * head_cols
    normed_f, inv_f, scaled_f = layer_norm(inputs_full, gain_row)
    values_f = jnp.dot(scaled_f, value_local, preferred_element_type=jnp.float32).astype(
        jnp.bfloat16
    )
    query_f = lax.dynamic_slice_in_dim(scaled_f, col_start, head_cols, 1)
    probs_f, low_f, context = local_attention(query_f, values_f)
    head_terms = jnp.dot(context, output_local, preferred_element_type=jnp.float32)
    normed_b, inv_b, scaled_b = layer_norm(saved_full, gain_row)
    values_b = jnp.dot(scaled_b, value_local, preferred_element_type=jnp.float32).astype(
        jnp.bfloat16
    )
    query_b = lax.dynamic_slice_in_dim(scaled_b, col_start, head_cols, 1)
    probs_b, low_b, unused_context = local_attention(query_b, values_b)
    grad_context = lax.dot_general(
        grad_full, output_local, (((1,), (1,)), ((), ())), preferred_element_type=jnp.float32
    ).astype(jnp.bfloat16)
    grad_values, grad_queries = local_attention_grad(
        query_b, values_b, probs_b, low_b, grad_context
    )
    grad_terms = lax.dot_general(
        grad_values, value_local, (((1,), (1,)), ((), ())), preferred_element_type=jnp.float32
    )
    current = lax.dynamic_slice_in_dim(grad_terms, col_start, head_cols, 1)
    grad_terms = lax.dynamic_update_slice_in_dim(grad_terms, current + grad_queries, col_start, 1)
    head_mix = lax.psum(head_terms.astype(jnp.bfloat16), "tp").astype(jnp.float32)
    layer_out = (inputs_full.astype(jnp.float32) + head_mix).astype(jnp.bfloat16)
    passed = shifted(layer_out, "section", 1)
    forwarded = lax.dynamic_slice_in_dim(passed, shard_start, shard_width, 1)
    grad_rows = lax.psum(grad_terms.astype(jnp.bfloat16), "tp").astype(jnp.float32)
    gain_grad_full = jnp.sum(grad_rows * normed_b, axis=0)
    grad_normed = grad_rows * gain_row
    first_mean = jnp.sum(grad_normed, axis=-1, keepdims=True) / full_width
    second_mean = jnp.sum(grad_normed * normed_b, axis=-1, keepdims=True) / full_width
    grad_inputs = (
        grad_full.astype(jnp.float32) + inv_b * (grad_normed - first_mean - normed_b * second_mean)
    ).astype(jnp.bfloat16)
    handed = shifted(grad_inputs, "section", -1)
    returned = lax.dynamic_slice_in_dim(handed, shard_start, shard_width, 1)
    gain_grad = lax.dynamic_slice_in_dim(gain_grad_full, shard_start, shard_width, 0)
    return (forwarded[None], returned[None], gain_grad[None], fetched_share[None])


def solution(mesh):
    return jax.shard_map(
        body,
        mesh=mesh,
        in_specs=(
            P("section", None, "tp"),
            P("section", None, "tp"),
            P("section", None, None, "tp"),
            P("section", None),
            P("section", None, "tp"),
            P("section", "tp", None),
            P(),
        ),
        out_specs=(
            P("section", None, "tp"),
            P("section", None, "tp"),
            P("section", "tp"),
            P("section", None, "tp"),
        ),
        check_vma=False,
    )
```

profile of v0, /device:TPU:96, one launch (start us, length us, event | category | flops | bytes accessed | tf_op | source)
XLA Modules:
  0.0 549.7 jit_solution(6959369266396372738)
XLA Ops:
  7.2 1.3 dynamic_slice.30
  10.5 0.8 constant_dynamic-slice_fusion.1
  11.3 44.8 %all-gather.11.cloned.1.call-done = bf16[1,1,256,6144]{3,2,1,0:T(8,128)(2,1)} async-done(((bf16[1,1,256,768]{3,2,1,0:T(8,128)(2,1)}), bf16[1,1,256,6144]{3,2,1,0:T(8,128)(2,1)}) %all-gather.11.cloned.1.call-update) | async-done | bytes 3145744 | tf_op jit(solution)/shard_map/all_gather | solution.py:93
  56.2 5.8 %collective-permute-done.1 = bf16[256,6144]{1,0:T(8,128)(2,1)S(1)} collective-permute-done((bf16[256,6144]{1,0:T(8,128)(2,1)}, bf16[256,6144]{1,0:T(8,128)(2,1)S(1)}, u32[]{:S(2)}, u32[]{:S(2)}) %collective-permute-start.1) | collective-permute-done | bytes 3145760 | tf_op jit(solution)/shard_map/ppermute | solution.py:15
  62.0 1.5 collective-permute-start.2
  63.5 68.8 %collective-permute-done.2 = bf16[256,6144]{1,0:T(8,128)(2,1)} collective-permute-done((bf16[256,6144]{1,0:T(8,128)(2,1)S(1)}, bf16[256,6144]{1,0:T(8,128)(2,1)}, u32[]{:S(2)}, u32[]{:S(2)}) %collective-permute-start.2) | collective-permute-done | bytes 3145760 | tf_op jit(solution)/shard_map/ppermute | solution.py:15
  132.2 3.0 collective-permute-start.3
  135.3 68.0 %collective-permute-done.3 = bf16[256,6144]{1,0:T(8,128)(2,1)} collective-permute-done((bf16[256,6144]{1,0:T(8,128)(2,1)}, bf16[256,6144]{1,0:T(8,128)(2,1)}, u32[]{:S(2)}, u32[]{:S(2)}) %collective-permute-start.3) | collective-permute-done | bytes 3145760 | tf_op jit(solution)/shard_map/ppermute | solution.py:15
  203.4 1.0 collective-permute-start.4
  204.4 0.6 iota_compare_fusion
  205.0 8.0 %fusion.61 = bf16[256,768]{1,0:T(8,128)(2,1)} fusion(bf16[1,768,6144]{2,1,0:T(8,128)(2,1)} %param.12, bf16[1,256,6144]{2,1,0:T(8,128)(2,1)} %all-gather.9.cloned.1.call-done), kind=kOutput, calls=%fused_computation.61 | convolution fusion | flops 2416115712 | bytes 12976128 | tf_op jit(solution)/shard_map/dot_general | solution.py:114
  213.0 1.2 copy.29
  214.2 3.4 convert_reduce_fusion
  217.6 55.9 %collective-permute-done.4 = bf16[256,6144]{1,0:T(8,128)(2,1)S(1)} collective-permute-done((bf16[256,6144]{1,0:T(8,128)(2,1)}, bf16[256,6144]{1,0:T(8,128)(2,1)S(1)}, u32[]{:S(2)}, u32[]{:S(2)}) %collective-permute-start.4) | collective-permute-done | bytes 3145760 | tf_op jit(solution)/shard_map/ppermute | solution.py:15
  273.5 1.7 copy-done.5
  275.2 3.7 fusion.25
  278.9 1.6 copy-done.6
  280.5 7.0 %fusion.55 = bf16[256,768]{1,0:T(8,128)(2,1)} fusion(bf16[256,6144]{1,0:T(8,128)(2,1)S(1)} %get-tuple-element.14, bf16[1,6144,768]{2,1,0:T(8,128)(2,1)} %param.11), kind=kOutput, calls=%fused_computation.59 | convolution fusion | flops 2416115712 | bytes 12976128 | tf_op jit(solution)/shard_map/dot_general | solution.py:102
  287.5 1.9 copy.24
  289.4 2.1 fusion.29
  291.5 7.1 %fusion.58 = bf16[256,768]{1,0:T(8,128)(2,1)} fusion(bf16[256,6144]{1,0:T(8,128)(2,1)S(1)} %fusion.29, bf16[1,6144,768]{2,1,0:T(8,128)(2,1)} %param.11), kind=kOutput, calls=%fused_computation.60 | convolution fusion | flops 2416115712 | bytes 12976128 | tf_op jit(solution)/shard_map/dot_general | solution.py:109
  298.6 1.9 constant_dynamic-slice_fusion
  300.5 1.9 copy.31
  302.4 1.9 copy.30
  304.4 1.9 copy.25
  306.3 2.5 fusion.82
  308.8 3.0 fusion.81
  311.8 2.7 fusion.66
  314.5 4.5 fusion.42
  319.0 3.8 fusion.52
  322.8 2.3 copy.39
  325.1 3.0 fusion.80
  328.1 1.8 convolution_convert_fusion
  329.9 8.0 %fusion.16 = bf16[256,6144]{1,0:T(8,128)(2,1)} fusion(bf16[256,768]{0,1:T(8,128)(2,1)S(1)} %bitcast.77, bf16[1,768,6144]{2,1,0:T(8,128)(2,1)} %param.12), kind=kOutput, calls=%fused_computation.25 | convolution fusion | flops 2417491968 | bytes 12976128 | tf_op jit(solution)/shard_map/dot_general | solution.py:107
  337.9 5.3 fusion.7
  343.2 0.1 add_dynamic-update-slice_fusion
  343.4 2.1 convert_element_type.90
  345.5 145.1 %all-reduce.3.cloned.1.call-done = (bf16[256,6144]{1,0:T(8,128)(2,1)}, bf16[256,6144]{1,0:T(8,128)(2,1)}) async-done(((bf16[256,6144]{1,0:T(8,128)(2,1)}, bf16[256,6144]{1,0:T(8,128)(2,1)}), (bf16[256,6144]{1,0:T(8,128)(2,1)}, bf16[256,6144]{1,0:T(8,128)(2,1)})) %all-reduce.3.cloned.1.call-update) | async-done | bytes 6291472 | tf_op jit(solution)/shard_map/psum | solution.py:125
  490.6 4.4 fusion.24
  495.0 3.1 fusion.22
  498.1 2.7 collective-permute-start.5
  500.8 1.2 fusion.34
  502.1 1.8 dynamic-slice_bitcast_fusion
  503.9 0.6 broadcast_in_dim.51
  504.5 31.1 %collective-permute-done.5 = bf16[256,6144]{1,0:T(8,128)(2,1)S(1)} collective-permute-done((bf16[256,6144]{1,0:T(8,128)(2,1)S(1)}, bf16[256,6144]{1,0:T(8,128)(2,1)S(1)}, u32[]{:S(2)}, u32[]{:S(2)}) %collective-permute-start.5) | collective-permute-done | bytes 3145760 | tf_op jit(solution)/shard_map/ppermute | solution.py:21
  535.6 0.8 dynamic-slice_bitcast_fusion.1
  536.4 6.0 %collective-permute-done = bf16[256,6144]{1,0:T(8,128)(2,1)S(1)} collective-permute-done((bf16[256,6144]{1,0:T(8,128)(2,1)S(1)}, bf16[256,6144]{1,0:T(8,128)(2,1)S(1)}, u32[]{:S(2)}, u32[]{:S(2)}) %collective-permute-start) | collective-permute-done | bytes 3145760 | tf_op jit(solution)/shard_map/ppermute | solution.py:21
  542.4 0.8 dynamic-slice_bitcast_fusion.2
  (37 shorter events, 0.5 us)
Async XLA Ops:
  7.2 3.3 copy-start
  7.2 48.9 %all-gather.11.cloned.1.call-start = ((), (), s32[]{:S(2)}) async-start(), calls=%async_computation.2 | async-start | bytes 3538944 | tf_op jit(solution)/shard_map/all_gather | solution.py:93
  11.3 193.7 %all-gather.9.cloned.1.call-start = ((), (), s32[]{:S(2)}) async-start(), calls=%async_computation.1 | async-start | bytes 3538944 | tf_op jit(solution)/shard_map/all_gather | solution.py:92
  56.1 5.9 %collective-permute-start.1 = (bf16[256,6144]{1,0:T(8,128)(2,1)}, bf16[256,6144]{1,0:T(8,128)(2,1)S(1)}, u32[]{:S(2)}, u32[]{:S(2)}) collective-permute-start(bf16[256,6144]{1,0:T(8,128)(2,1)} %bitcast.87), channel_id=1, source_target_pairs={{0,8},{8,0},{16,24},{24,16},{32,40},{40,32},{48,56},{56,48},{64,72... | collective-permute-start | bytes 9437192 | tf_op jit(solution)/shard_map/ppermute | solution.py:15
  56.2 158.1 %all-gather.7.cloned.1.call-start = ((), (), s32[]{:S(2)}) async-start(), calls=%async_computation | async-start | bytes 3538944 | tf_op jit(solution)/shard_map/all_gather | solution.py:91
  62.0 70.2 %collective-permute-start.2 = (bf16[256,6144]{1,0:T(8,128)(2,1)S(1)}, bf16[256,6144]{1,0:T(8,128)(2,1)}, u32[]{:S(2)}, u32[]{:S(2)}) collective-permute-start(bf16[256,6144]{1,0:T(8,128)(2,1)S(1)} %collective-permute-done.1), channel_id=1, source_target_pairs={{0,16},{8,24},{16,0},{24,8},{32,48},{40,56},{48,32},{56,40},{64,80... | collective-permute-start | bytes 9437192 | tf_op jit(solution)/shard_map/ppermute | solution.py:15
  132.2 71.1 %collective-permute-start.3 = (bf16[256,6144]{1,0:T(8,128)(2,1)}, bf16[256,6144]{1,0:T(8,128)(2,1)}, u32[]{:S(2)}, u32[]{:S(2)}) collective-permute-start(bf16[256,6144]{1,0:T(8,128)(2,1)} %collective-permute-done.2), channel_id=1, source_target_pairs={{0,32},{8,40},{16,48},{24,56},{32,0},{40,8},{48,16},{56,24},{64,96... | collective-permute-start | bytes 9437192 | tf_op jit(solution)/shard_map/ppermute | solution.py:15
  135.3 355.3 %all-reduce.3.cloned.1.call-start = ((), (), s32[]{:S(2)}) async-start(), calls=%async_computation.3 | async-start | bytes 12582912 | tf_op jit(solution)/shard_map/psum | solution.py:125
  203.4 70.1 %collective-permute-start.4 = (bf16[256,6144]{1,0:T(8,128)(2,1)}, bf16[256,6144]{1,0:T(8,128)(2,1)S(1)}, u32[]{:S(2)}, u32[]{:S(2)}) collective-permute-start(bf16[256,6144]{1,0:T(8,128)(2,1)} %collective-permute-done.3), channel_id=1, source_target_pairs={{0,64},{8,72},{16,80},{24,88},{32,96},{40,104},{48,112},{56,120},{... | collective-permute-start | bytes 9437192 | tf_op jit(solution)/shard_map/ppermute | solution.py:15
  214.2 61.0 %copy-start.2 = (bf16[1,256,6144]{2,1,0:T(8,128)(2,1)S(1)}, bf16[1,256,6144]{2,1,0:T(8,128)(2,1)}, u32[]{:S(2)}) copy-start(bf16[1,256,6144]{2,1,0:T(8,128)(2,1)} %all-gather.7.cloned.1.call-done) | copy-start | bytes 9437188
  273.5 1.7 copy-start.5
  278.9 1.6 copy-start.6
  337.9 5.3 copy-start.7
  345.5 145.1 %copy-start.10 = (f32[1,6144]{1,0:T(1,128)S(1)}, f32[1,6144]{1,0:T(1,128)}, u32[]{:S(2)}) copy-start(f32[1,6144]{1,0:T(1,128)} %param.10) | copy-start | bytes 73732
  490.6 4.4 copy-start.4
  490.6 4.4 copy-start.8
  495.0 5.8 %copy-start.3 = (bf16[1,256,6144]{2,1,0:T(8,128)(2,1)S(1)}, bf16[1,256,6144]{2,1,0:T(8,128)(2,1)}, u32[]{:S(2)}) copy-start(bf16[1,256,6144]{2,1,0:T(8,128)(2,1)} %all-gather.7.cloned.1.call-done) | copy-start | bytes 9437188
  495.0 5.8 %copy-start.9 = (bf16[256,6144]{1,0:T(8,128)(2,1)S(1)}, bf16[256,6144]{1,0:T(8,128)(2,1)}, u32[]{:S(2)}) copy-start(bf16[256,6144]{1,0:T(8,128)(2,1)} %get-tuple-element.11) | copy-start | bytes 9437188
  498.1 37.5 %collective-permute-start.5 = (bf16[256,6144]{1,0:T(8,128)(2,1)S(1)}, bf16[256,6144]{1,0:T(8,128)(2,1)S(1)}, u32[]{:S(2)}, u32[]{:S(2)}) collective-permute-start(bf16[256,6144]{1,0:T(8,128)(2,1)S(1)} %fusion.22), channel_id=1, source_target_pairs={{8,0},{16,8},{24,16},{32,24},{40,32},{48,40},{56,48},{64,56},{72,6... | collective-permute-start | bytes 9437192 | tf_op jit(solution)/shard_map/ppermute | solution.py:21
  500.8 42.4 %copy-start.1 = (bf16[1,2,256,768]{3,2,1,0:T(8,128)(2,1)S(1)}, bf16[1,2,256,768]{3,2,1,0:T(8,128)(2,1)}, u32[]{:S(2)}) copy-start(bf16[1,2,256,768]{3,2,1,0:T(8,128)(2,1)} %param.9) | copy-start | bytes 2359300
  502.0 40.4 %collective-permute-start = (bf16[256,6144]{1,0:T(8,128)(2,1)S(1)}, bf16[256,6144]{1,0:T(8,128)(2,1)S(1)}, u32[]{:S(2)}, u32[]{:S(2)}) collective-permute-start(bf16[256,6144]{1,0:T(8,128)(2,1)S(1)} %fusion.34), channel_id=1, source_target_pairs={{120,0},{0,8},{8,16},{16,24},{24,32},{32,40},{40,48},{48,56},{56,6... | collective-permute-start | bytes 9437192 | tf_op jit(solution)/shard_map/ppermute | solution.py:21
Sparse Core Ops, SparseCore 0:
  11.4 44.6 all-gather.10
  57.8 43.8 all-gather.8
  135.4 42.0 all-gather.6
  345.6 144.8 all-reduce.2
where the time goes:
time: 554 us; the launch traced here: 550 us
  waiting for transfers between devices  425 us (77%)
  matrix products  56.7 us (10%)
  local copies, waits for them, and re-layouts  22.5 us (4%)
  other arithmetic  20.7 us (4%)
  between operations  15.9 us (3%)
  starting transfers between devices  8.39 us (2%)
    ppermute x4, waiting for transfers between devices, partner_2(): lax.ppermute(value, axis, [(i, i ^ 1 << apart) for i in range(lax.axis_si...  198 us
    psum x1, waiting for transfers between devices, body(): lax.psum(head_terms.astype(jnp.bfloat16), 'tp').astype(jnp.float32)  145 us
    all_gather x1, waiting for transfers between devices, body(): lax.all_gather(outgoing, 'tp', axis=1, tiled=True)  44.8 us
    ppermute x2, waiting for transfers between devices, shifted(): return lax.ppermute(block, axis, route)  37.1 us
  transfers between devices with their start and end apart: 10, of which 8 were waited for; matrix products, arithmetic and copies ran while one was open for 3% of the time, Pallas kernels for 0%

commit v1 on v0

--- a/solution.py
+++ b/solution.py
@@ -9,10 +9,6 @@
 
 
 EPS = 1e-05
-
-
-def partner_2(value, axis, apart):
-    return lax.ppermute(value, axis, [(i, i ^ 1 << apart) for i in range(lax.axis_size(axis))])
 
 
 def shifted(block, axis, distance):
@@ -74,7 +70,6 @@
     sections = lax.axis_size("section")
     position = lax.axis_index("section")
     tp_rank = lax.axis_index("tp")
-    levels = sections.bit_length() - 1
     own_rows = arriving[0]
     own_grad = cotangent[0]
     shard_width = own_rows.shape[1]
@@ -86,18 +81,15 @@
     send_slot = fetch_slot[partner]
     outgoing = lax.dynamic_index_in_dim(evicted[0], send_slot, 0, keepdims=False)
     is_early = position < sections // 2
-    shard_start = tp_rank * shard_width
-    inputs_full, grad_full, travelling = (
-        lax.all_gather(own_rows, "tp", axis=1, tiled=True),
-        lax.all_gather(own_grad, "tp", axis=1, tiled=True),
-        lax.all_gather(outgoing, "tp", axis=1, tiled=True),
+    col_start = tp_rank * shard_width
+    fetched_share = lax.ppermute(
+        outgoing, "section", [(i, sections - 1 - i) for i in range(sections)]
     )
-    for bit_index in range(levels):
-        travelling = partner_2(travelling, "section", bit_index)
-    fetched_share = lax.dynamic_slice_in_dim(travelling, shard_start, shard_width, 1)
-    saved_full = jnp.where(is_early, travelling, inputs_full)
+    saved_share = jnp.where(is_early, fetched_share, own_rows)
+    inputs_full = lax.all_gather(own_rows, "tp", axis=1, tiled=True)
+    grad_full = lax.all_gather(own_grad, "tp", axis=1, tiled=True)
+    saved_full = lax.all_gather(saved_share, "tp", axis=1, tiled=True)
     full_width = inputs_full.shape[1]
-    col_start = tp_rank * head_cols
     normed_f, inv_f, scaled_f = layer_norm(inputs_full, gain_row)
     values_f = jnp.dot(scaled_f, value_local, preferred_element_type=jnp.float32).astype(
         jnp.bfloat16
@@ -105,6 +97,11 @@
     query_f = lax.dynamic_slice_in_dim(scaled_f, col_start, head_cols, 1)
     probs_f, low_f, context = local_attention(query_f, values_f)
     head_terms = jnp.dot(context, output_local, preferred_element_type=jnp.float32)
+    head_mix = lax.psum_scatter(
+        head_terms.astype(jnp.bfloat16), "tp", scatter_dimension=1, tiled=True
+    ).astype(jnp.float32)
+    layer_out = (own_rows.astype(jnp.float32) + head_mix).astype(jnp.bfloat16)
+    forwarded = shifted(layer_out, "section", 1)
     normed_b, inv_b, scaled_b = layer_norm(saved_full, gain_row)
     values_b = jnp.dot(scaled_b, value_local, preferred_element_type=jnp.float32).astype(
         jnp.bfloat16
@@ -122,21 +119,23 @@
     )
     current = lax.dynamic_slice_in_dim(grad_terms, col_start, head_cols, 1)
     grad_terms = lax.dynamic_update_slice_in_dim(grad_terms, current + grad_queries, col_start, 1)
-    head_mix = lax.psum(head_terms.astype(jnp.bfloat16), "tp").astype(jnp.float32)
-    layer_out = (inputs_full.astype(jnp.float32) + head_mix).astype(jnp.bfloat16)
-    passed = shifted(layer_out, "section", 1)
-    forwarded = lax.dynamic_slice_in_dim(passed, shard_start, shard_width, 1)
-    grad_rows = lax.psum(grad_terms.astype(jnp.bfloat16), "tp").astype(jnp.float32)
-    gain_grad_full = jnp.sum(grad_rows * normed_b, axis=0)
-    grad_normed = grad_rows * gain_row
-    first_mean = jnp.sum(grad_normed, axis=-1, keepdims=True) / full_width
-    second_mean = jnp.sum(grad_normed * normed_b, axis=-1, keepdims=True) / full_width
+    grad_own = lax.psum_scatter(
+        grad_terms.astype(jnp.bfloat16), "tp", scatter_dimension=1, tiled=True
+    ).astype(jnp.float32)
+    normed_own = lax.dynamic_slice_in_dim(normed_b, col_start, shard_width, 1)
+    gain_own = lax.dynamic_slice_in_dim(gain_row, col_start, shard_width, 0)
+    gain_grad = jnp.sum(grad_own * normed_own, axis=0)
+    grad_normed = grad_own * gain_own
+    sums = jnp.stack(
+        [jnp.sum(grad_normed, axis=-1), jnp.sum(grad_normed * normed_own, axis=-1)]
+    )
+    sums = lax.psum(sums, "tp") / full_width
+    first_mean = sums[0][:, None]
+    second_mean = sums[1][:, None]
     grad_inputs = (
-        grad_full.astype(jnp.float32) + inv_b * (grad_normed - first_mean - normed_b * second_mean)
+        own_grad.astype(jnp.float32) + inv_b * (grad_normed - first_mean - normed_own * second_mean)
     ).astype(jnp.bfloat16)
-    handed = shifted(grad_inputs, "section", -1)
-    returned = lax.dynamic_slice_in_dim(handed, shard_start, shard_width, 1)
-    gain_grad = lax.dynamic_slice_in_dim(gain_grad_full, shard_start, shard_width, 0)
+    returned = shifted(grad_inputs, "section", -1)
     return (forwarded[None], returned[None], gain_grad[None], fetched_share[None])
 
 

time: 554 us -> 285 us (0.51)
  waiting for transfers between devices: 425 us -> 163 us
  blocking collectives: 0 us -> 18.3 us
  local copies, waits for them, and re-layouts: 22.5 us -> 11.3 us
  matrix products: 56.7 us -> 46.3 us
    ppermute x4 -> x1, waiting for transfers between devices: 198 us -> 15.5 us  [body(): lax.ppermute(outgoing, 'section', [(i, sections - 1 - i) for i in range(s...]
    psum x1 -> x0, waiting for transfers between devices: 145 us -> none  [body(): lax.psum(head_terms.astype(jnp.bfloat16), 'tp').astype(jnp.float32)]
    reduce_scatter x0 -> x2, waiting for transfers between devices: none -> 56.2 us  [the longest x1 46.7 us: body(): lax.psum_scatter(grad_terms.astype(jnp.bfloat16), 'tp', scatter_dimension...]
    all_gather x3, waiting for transfers between devices: 44.8 us -> 84.7 us  [the longest x1 42.6 us: body(): saved_full = lax.all_gather(saved_share, 'tp', axis=1, tiled=True)]
    ppermute x2, waiting for transfers between devices: 37.1 us -> 4.71 us  [shifted(): return lax.ppermute(block, axis, route)]
    psum x0 -> x1, blocking collectives: none -> 18.3 us  [body(): sums = lax.psum(sums, 'tp') / full_width]
    mul x0 -> x1, other arithmetic: none -> 6.96 us  [layer_norm(): normed = (values - centre) * inv_std]
  transfers between devices with their start and end apart: 10 -> 8, of which waited for: 8 -> 7; matrix products, arithmetic and copies ran while one was open for 3% -> 27% of each run, Pallas kernels for 0% -> 0%
where the time goes in v1:
time: 285 us; the launch traced here: 279 us
  waiting for transfers between devices  163 us (57%)
  matrix products  46.3 us (16%)
  other arithmetic  21.8 us (8%)
  blocking collectives  18.3 us (6%)
  between operations  16 us (6%)
  local copies, waits for them, and re-layouts  11.3 us (4%)
  starting transfers between devices  3.05 us (1%)
    reduce_scatter x1, waiting for transfers between devices, body(): lax.psum_scatter(grad_terms.astype(jnp.bfloat16), 'tp', scatter_dimension...  46.7 us
    all_gather x1, waiting for transfers between devices, body(): saved_full = lax.all_gather(saved_share, 'tp', axis=1, tiled=True)  42.6 us
    all_gather x1, waiting for transfers between devices, body(): inputs_full = lax.all_gather(own_rows, 'tp', axis=1, tiled=True)  24.4 us
    psum x1, blocking collectives, body(): sums = lax.psum(sums, 'tp') / full_width  18.3 us
    all_gather x1, waiting for transfers between devices, body(): grad_full = lax.all_gather(own_grad, 'tp', axis=1, tiled=True)  17.8 us
    ppermute x1, waiting for transfers between devices, body(): lax.ppermute(outgoing, 'section', [(i, sections - 1 - i) for i in range(s...  15.5 us
    reduce_scatter x1, waiting for transfers between devices, body(): lax.psum_scatter(head_terms.astype(jnp.bfloat16), 'tp', scatter_dimension...  9.55 us
    dot_general x1, matrix products, body(): jnp.dot(context, output_local, preferred_element_type=jnp.float32)  7.93 us
  transfers between devices with their start and end apart: 8, of which 7 were waited for; matrix products, arithmetic and copies ran while one was open for 27% of the time, Pallas kernels for 0%

profile of v1, /device:TPU:96, one launch (start us, length us, event | category | flops | bytes accessed | tf_op | source)
XLA Modules:
  0.0 279.2 jit_solution(3148060492771171044)
XLA Ops:
  7.2 0.7 all-gather.8.cloned.1.call-update
  8.0 1.2 dynamic_slice.23
  11.2 2.5 collective-permute-start.1
  13.7 15.5 %collective-permute-done.1 = bf16[256,768]{1,0:T(8,128)(2,1)S(1)} collective-permute-done((bf16[256,768]{1,0:T(8,128)(2,1)S(1)}, bf16[256,768]{1,0:T(8,128)(2,1)S(1)}, u32[]{:S(2)}, u32[]{:S(2)}) %collective-permute-start.1) | collective-permute-done | bytes 393248 | tf_op jit(solution)/shard_map/ppermute | solution.py:85
  29.2 1.8 bitcast_select_fusion
  31.1 0.7 all-gather.10.cloned.1.call-update
  31.9 24.4 %all-gather.8.cloned.1.call-done = bf16[1,256,6144]{2,1,0:T(8,128)(2,1)} async-done(((bf16[1,256,768]{2,1,0:T(8,128)(2,1)}), bf16[1,256,6144]{2,1,0:T(8,128)(2,1)}) %all-gather.8.cloned.1.call-update) | async-done | bytes 3145744 | tf_op jit(solution)/shard_map/all_gather | solution.py:89
  56.2 2.5 convert_reduce_fusion.1
  58.8 0.3 copy-done.2
  59.1 0.7 fusion.18
  59.8 42.6 %all-gather.6.cloned.1.call-done = bf16[256,6144]{1,0:T(8,128)(2,1)} async-done(((bf16[256,768]{1,0:T(8,128)(2,1)}), bf16[256,6144]{1,0:T(8,128)(2,1)}) %all-gather.6.cloned.1.call-update) | async-done | bytes 3145744 | tf_op jit(solution)/shard_map/all_gather | solution.py:91
  102.4 3.4 %convert_reduce_fusion = (f32[256]{0:T(256)S(1)}, f32[256]{0:T(256)S(1)}) fusion(bf16[256,6144]{1,0:T(8,128)(2,1)} %all-gather.6.cloned.1.call-done), kind=kLoop, calls=%fused_computation.4 | loop fusion | flops 6290944 | bytes 3147776 | tf_op jit(solution)/shard_map/reduce_sum | solution.py:23
  105.8 7.0 %fusion.23 = (f32[256,6144]{1,0:T(8,128)}, bf16[256,6144]{1,0:T(8,128)(2,1)}, bf16[256,6144]{1,0:T(8,128)(2,1)S(1)}) fusion(bf16[256,6144]{1,0:T(8,128)(2,1)} %all-gather.6.cloned.1.call-done, f32[256]{0:T(256)S(1)} %get-tuple-element.15, f32[256]{0:T(256)S(1)} %get-tuple-element.14, f32[6144]{0:T(1024)S(1)} %bitcast.102, f32[256]{0:T(256)S(1)} %get-tuple-element.17, ...), kind=kLoop, calls=%fused_computation.26 | loop fusion | flops 15728640 | bytes 18903040 | tf_op jit(solution)/shard_map/mul | solution.py:26
  112.8 1.7 copy-done.3
  114.5 2.6 fusion.44
  117.1 0.2 copy.24
  117.3 1.0 constant_dynamic-slice_fusion.1
  118.3 0.2 copy.25
  118.5 1.8 fusion.79
  120.3 1.7 convolution_convert_fusion
  122.0 7.9 %fusion.15 = bf16[256,6144]{1,0:T(8,128)(2,1)} fusion(bf16[256,768]{0,1:T(8,128)(2,1)S(1)} %bitcast.94, bf16[1,768,6144]{2,1,0:T(8,128)(2,1)} %param.12), kind=kOutput, calls=%fused_computation.20 | convolution fusion | flops 2417491968 | bytes 12976128 | tf_op jit(solution)/shard_map/dot_general | solution.py:99
  130.0 0.2 reduce-scatter.5.cloned.1.call-start
  130.2 17.8 %all-gather.10.cloned.1.call-done = bf16[1,256,6144]{2,1,0:T(8,128)(2,1)} async-done(((bf16[1,256,768]{2,1,0:T(8,128)(2,1)}), bf16[1,256,6144]{2,1,0:T(8,128)(2,1)}) %all-gather.10.cloned.1.call-update) | async-done | bytes 3145744 | tf_op jit(solution)/shard_map/all_gather | solution.py:90
  148.0 7.3 %fusion.50 = bf16[256,768]{1,0:T(8,128)(2,1)S(1)} fusion(bf16[1,768,6144]{2,1,0:T(8,128)(2,1)} %param.12, bf16[1,256,6144]{2,1,0:T(8,128)(2,1)} %all-gather.10.cloned.1.call-done), kind=kOutput, calls=%fused_computation.46 | convolution fusion | flops 2416115712 | bytes 12976128 | tf_op jit(solution)/shard_map/dot_general | solution.py:111
  155.2 0.2 copy.29
  155.4 1.0 constant_dynamic-slice_fusion
  156.6 7.5 %fusion.47 = bf16[256,768]{1,0:T(8,128)(2,1)S(1)} fusion(bf16[256,6144]{1,0:T(8,128)(2,1)} %get-tuple-element.10, bf16[1,6144,768]{2,1,0:T(8,128)(2,1)} %param.11), kind=kOutput, calls=%fused_computation.45 | convolution fusion | flops 2416115712 | bytes 12976128 | tf_op jit(solution)/shard_map/dot_general | solution.py:106
  164.3 0.4 fusion.81
  164.8 2.7 fusion.80
  167.5 3.4 %fusion.31 = f32[6,128,256]{2,1,0:T(8,128)} fusion(bf16[256,6,128]{0,2,1:T(8,128)(2,1)S(1)} %bitcast.90, f32[6,256,256]{1,2,0:T(8,128)S(1)} %fusion.81, f32[6,256,256]{1,2,0:T(8,128)} %get-tuple-element.21, f32[6,256]{1,0:T(8,128)S(1)} %get-tuple-element.20), kind=kOutput, calls=%fused_computation.37 | convolution fusion | flops 103417600 | bytes 4331520 | tf_op jit(solution)/shard_map/hqk,khd->qhd/dot_general | solution.py:65
  170.9 1.4 copy.39
  172.3 2.7 fusion.64
  175.0 2.8 fusion.41
  177.8 5.4 %fusion.7 = f32[256,6144]{1,0:T(8,128)S(1)} fusion(bf16[256,768]{0,1:T(8,128)(2,1)S(1)} %bitcast.93, bf16[1,6144,768]{2,1,0:T(8,128)(2,1)} %param.11), kind=kOutput, calls=%fused_computation.10 | convolution fusion | flops 2415919104 | bytes 16121856 | tf_op jit(solution)/shard_map/dot_general | solution.py:117
  183.2 0.2 add_dynamic-update-slice_fusion
  183.4 2.0 convert_element_type.93
  185.4 0.8 dynamic-slice_reduce_fusion
  186.3 9.5 %reduce-scatter.3.cloned.1.call-done = bf16[256,768]{1,0:T(8,128)(2,1)} async-done(((bf16[256,6144]{1,0:T(8,128)(2,1)}), bf16[256,768]{1,0:T(8,128)(2,1)}) %reduce-scatter.3.cloned.1.call-update) | async-done | bytes 393232 | tf_op jit(solution)/shard_map/reduce_scatter | solution.py:100
  195.8 1.1 add_convert_fusion
  197.0 46.7 %reduce-scatter.5.cloned.1.call-done = bf16[256,768]{1,0:T(8,128)(2,1)} async-done(((bf16[256,6144]{1,0:T(8,128)(2,1)}), bf16[256,768]{1,0:T(8,128)(2,1)}) %reduce-scatter.5.cloned.1.call-update) | async-done | bytes 393232 | tf_op jit(solution)/shard_map/reduce_scatter | solution.py:122
  243.7 1.6 fusion.63
  245.3 18.3 %psum.7 = f32[2,256]{1,0:T(2,128)S(1)} all-reduce(f32[2,256]{1,0:T(2,128)S(1)} %pad_maximum_fusion), channel_id=1, replica_groups=mesh['section'=16,'tp'=8] {'tp'}, use_global_device_ids=true, to_apply=%region_13.14 | all-reduce | flops 512 | bytes 4096 | tf_op jit(solution)/shard_map/psum | solution.py:132
  263.6 1.5 fusion.62
  265.2 0.6 broadcast_in_dim.50
  265.8 4.7 %collective-permute-done.2 = bf16[256,768]{1,0:T(8,128)(2,1)S(1)} collective-permute-done((bf16[256,768]{1,0:T(8,128)(2,1)S(1)}, bf16[256,768]{1,0:T(8,128)(2,1)S(1)}, u32[]{:S(2)}, u32[]{:S(2)}) %collective-permute-start.2) | collective-permute-done | bytes 393248 | tf_op jit(solution)/shard_map/ppermute | solution.py:17
  270.5 0.7 copy.54
  271.2 0.7 copy.55
  272.0 0.7 copy.56
  (40 shorter events, 0.9 us)
Async XLA Ops:
  7.2 4.0 %copy-start = (bf16[1,2,256,768]{3,2,1,0:T(8,128)(2,1)S(1)}, bf16[1,2,256,768]{3,2,1,0:T(8,128)(2,1)}, u32[]{:S(2)}) copy-start(bf16[1,2,256,768]{3,2,1,0:T(8,128)(2,1)} %param.9) | copy-start | bytes 2359300
  7.2 49.0 %all-gather.8.cloned.1.call-start = ((), (), s32[]{:S(2)}) async-start(), calls=%async_computation.5 | async-start | bytes 3538944 | tf_op jit(solution)/shard_map/all_gather | solution.py:89
  7.9 94.5 %all-gather.6.cloned.1.call-start = ((), (), s32[]{:S(2)}) async-start(), calls=%async_computation.3 | async-start | bytes 3538944 | tf_op jit(solution)/shard_map/all_gather | solution.py:91
  11.2 18.0 %collective-permute-start.1 = (bf16[256,768]{1,0:T(8,128)(2,1)S(1)}, bf16[256,768]{1,0:T(8,128)(2,1)S(1)}, u32[]{:S(2)}, u32[]{:S(2)}) collective-permute-start(bf16[256,768]{1,0:T(8,128)(2,1)S(1)} %dynamic-slice_bitcast_fusion), channel_id=1, source_target_pairs={{0,120},{8,112},{16,104},{24,96},{32,88},{40,80},{48,72},{56,64},{... | collective-permute-start | bytes 1179656 | tf_op jit(solution)/shard_map/ppermute | solution.py:85
  31.0 116.9 %all-gather.10.cloned.1.call-start = ((), (), s32[]{:S(2)}) async-start(), calls=%async_computation.6 | async-start | bytes 3538944 | tf_op jit(solution)/shard_map/all_gather | solution.py:90
  31.8 164.0 %reduce-scatter.3.cloned.1.call-start = ((), (), s32[]{:S(2)}) async-start(), calls=%async_computation.2 | async-start | bytes 3538944 | tf_op jit(solution)/shard_map/reduce_scatter | solution.py:100
  31.8 86.6 %copy-start.6 = (pred[256,256]{0,1:T(8,128)(4,1)}, pred[256,256]{0,1:T(8,128)(4,1)S(1)}, u32[]{:S(2)}) copy-start(pred[256,256]{0,1:T(8,128)(4,1)S(1)} %iota_compare_fusion) | copy-start | bytes 196612
  56.2 2.8 %copy-start.2 = (bf16[1,256,6144]{2,1,0:T(8,128)(2,1)S(1)}, bf16[1,256,6144]{2,1,0:T(8,128)(2,1)}, u32[]{:S(2)}) copy-start(bf16[1,256,6144]{2,1,0:T(8,128)(2,1)} %all-gather.8.cloned.1.call-done) | copy-start | bytes 9437188
  59.1 46.7 %copy-start.7 = (f32[1,6144]{1,0:T(1,128)S(1)}, f32[1,6144]{1,0:T(1,128)}, u32[]{:S(2)}) copy-start(f32[1,6144]{1,0:T(1,128)} %param.10) | copy-start | bytes 73732
  102.4 12.1 %slice-start = ((s8[9437184]{0:T(1024)(128)(4,1)}), s8[4194304]{0:T(1024)(128)(4,1)S(1)}, s32[]{:S(2)}) async-start(s8[9437184]{0:T(1024)(128)(4,1)} %bitcast.84), calls=%async_computation.7 | async-start | bytes 8388608
  105.8 8.7 %slice-start.1 = ((s8[9437184]{0:T(1024)(128)(4,1)}), s8[4194304]{0:T(1024)(128)(4,1)S(1)}, s32[]{:S(2)}) async-start(s8[9437184]{0:T(1024)(128)(4,1)} %bitcast.84), calls=%async_computation.8 | async-start | bytes 8388608
  105.8 8.7 %slice-start.2 = ((s8[9437184]{0:T(1024)(128)(4,1)}), s8[1048576]{0:T(1024)(128)(4,1)S(1)}, s32[]{:S(2)}) async-start(s8[9437184]{0:T(1024)(128)(4,1)} %bitcast.84), calls=%async_computation.9 | async-start | bytes 2097152
  112.8 1.7 copy-start.3
  130.0 113.7 %reduce-scatter.5.cloned.1.call-start = ((), (), s32[]{:S(2)}) async-start(), calls=%async_computation.4 | async-start | bytes 3538944 | tf_op jit(solution)/shard_map/reduce_scatter | solution.py:122
  185.4 10.4 %copy-start.4 = (bf16[1,256,768]{2,1,0:T(8,128)(2,1)S(1)}, bf16[1,256,768]{2,1,0:T(8,128)(2,1)}, u32[]{:S(2)}) copy-start(bf16[1,256,768]{2,1,0:T(8,128)(2,1)} %param.7) | copy-start | bytes 1179652
  185.4 78.2 %copy-start.5 = (bf16[1,256,768]{2,1,0:T(8,128)(2,1)S(1)}, bf16[1,256,768]{2,1,0:T(8,128)(2,1)}, u32[]{:S(2)}) copy-start(bf16[1,256,768]{2,1,0:T(8,128)(2,1)} %param.8) | copy-start | bytes 1179652
  185.4 87.3 %copy-start.1 = (bf16[1,2,256,768]{3,2,1,0:T(8,128)(2,1)S(1)}, bf16[1,2,256,768]{3,2,1,0:T(8,128)(2,1)}, u32[]{:S(2)}) copy-start(bf16[1,2,256,768]{3,2,1,0:T(8,128)(2,1)} %param.9) | copy-start | bytes 2359300
  196.9 68.9 %collective-permute-start = (bf16[256,768]{1,0:T(8,128)(2,1)S(1)}, bf16[256,768]{1,0:T(8,128)(2,1)S(1)}, u32[]{:S(2)}, u32[]{:S(2)}) collective-permute-start(bf16[256,768]{1,0:T(8,128)(2,1)S(1)} %add_convert_fusion), channel_id=1, source_target_pairs={{120,0},{0,8},{8,16},{16,24},{24,32},{32,40},{40,48},{48,56},{56,6... | collective-permute-start | bytes 1179656 | tf_op jit(solution)/shard_map/ppermute | solution.py:17
  265.1 5.4 %collective-permute-start.2 = (bf16[256,768]{1,0:T(8,128)(2,1)S(1)}, bf16[256,768]{1,0:T(8,128)(2,1)S(1)}, u32[]{:S(2)}, u32[]{:S(2)}) collective-permute-start(bf16[256,768]{1,0:T(8,128)(2,1)S(1)} %fusion.62), channel_id=1, source_target_pairs={{8,0},{16,8},{24,16},{32,24},{40,32},{48,40},{56,48},{64,56},{72,6... | collective-permute-start | bytes 1179656 | tf_op jit(solution)/shard_map/ppermute | solution.py:17
Sparse Core Ops, SparseCore 0:
  9.7 46.5 all-gather.7
  58.4 43.8 all-gather.5
  104.0 43.8 all-gather.9
  150.2 45.5 reduce-scatter.2
  198.1 45.5 reduce-scatter.4

commit v2 on v0

v2 whole, which is shorter than its diff:
```python
import functools
import math

import jax
import jax.numpy as jnp
from jax import lax
from jax.experimental import pallas as pl
from jax.experimental.pallas import tpu as pltpu
from jax.sharding import PartitionSpec as P

HD = 128
EPS = 1e-05
RING = 4
PEERS = 8
MESH = pl.DeviceIdType.MESH
BF16 = jnp.bfloat16
F32 = jnp.float32
NT = (((1,), (1,)), ((), ()))
NN = (((1,), (0,)), ((), ()))
TN = (((0,), (0,)), ((), ()))


def dot(a, b, dims):
    return lax.dot_general(a, b, dims, preferred_element_type=F32)


def kernel(
    sections,
    arr_ref,
    cot_ref,
    out_ref,
    gain_ref,
    wv_ref,
    wo_ref,
    fwd_ref,
    ret_ref,
    fet_ref,
    gg_ref,
    wv,
    wo,
    cots,
    rows_b,
    rows_f,
    part_g,
    part_h,
    in_g,
    in_h,
    acc,
    grad_ctx,
    val_b,
    val_f,
    grad_val,
    grad_q,
    ctx,
    arr,
    fet,
    normed,
    inv_col,
    stat_out,
    stat_in,
    y_buf,
    dx_buf,
    loc_sem,
    ag_send,
    ag_recv,
    rs_send,
    rs_recv,
    st_send,
    st_recv,
    far_send,
    far_recv,
):
    length, width = arr.shape
    half = length // 2
    heads = width // HD
    full = PEERS * width
    tile = min(256, width)
    section = lax.axis_index("section")
    rank = lax.axis_index("tp")
    x = rank % RING
    z = rank // RING
    early = section < sections // 2

    def at(dx, dz):
        return lax.rem(z + dz, 2) * RING + lax.rem(x + dx + RING, RING)

    def peer(dx, dz):
        return (section, at(dx, dz))

    def remote(src, dst, ssem, rsem, device):
        return pltpu.make_async_remote_copy(
            src_ref=src,
            dst_ref=dst,
            send_sem=ssem,
            recv_sem=rsem,
            device_id=device,
            device_id_type=MESH,
        )

    me = at(0, 0)
    next_section = (lax.rem(section + 1, sections), rank)
    prev_section = (lax.rem(section + sections - 1, sections), rank)
    mirror = (sections - 1 - section, rank)

    load_cot = pltpu.make_async_copy(cot_ref, cots.at[me], loc_sem.at[0])
    load_arr = pltpu.make_async_copy(arr_ref, arr, loc_sem.at[1])
    load_wo = pltpu.make_async_copy(wo_ref, wo, loc_sem.at[2])
    load_wv = pltpu.make_async_copy(wv_ref, wv, loc_sem.at[3])
    load_cot.start()
    load_arr.start()
    load_wo.start()
    load_wv.start()

    barrier = pltpu.get_barrier_semaphore()
    for step in range(1, PEERS):
        pl.semaphore_signal(
            barrier, inc=1, device_id=(section, lax.rem(rank + step, PEERS)), device_id_type=MESH
        )
    for device in (next_section, prev_section, mirror):
        pl.semaphore_signal(barrier, inc=1, device_id=device, device_id_type=MESH)
    pl.semaphore_wait(barrier, PEERS + 2)

    send_far = remote(out_ref, fet, far_send.at[0], far_recv.at[0], mirror)
    send_far.start()

    def gather_edge(buf, g, e, h, landing=False):
        p = 1 - 2 * h
        block, device, landed = (
            ((0, 0), (p, 0), (-p, 0)),
            ((0, 0), (-p, 0), (p, 0)),
            ((0, 0), (0, 1), (0, 1)),
            ((-p, 0), (p, 0), (2, 0)),
            ((2, 0), (0, 1), (2, 1)),
            ((0, 1), (p, 0), (-p, 1)),
            ((0, 1), (-p, 0), (p, 1)),
        )[e]
        rows = buf.at[at(*(landed if landing else block)), pl.ds(h * half, half)]
        return remote(rows, rows, ag_send.at[g, h, e], ag_recv.at[g, h, e], peer(*device))

    def gather_send(buf, g, edges):
        for e in edges:
            for h in range(2):
                gather_edge(buf, g, e, h).start()

    def gather_wait(buf, g, edges):
        for e in edges:
            for h in range(2):
                gather_edge(buf, g, e, h, True).wait_recv()

    def gather_relay(buf, g, e, onward):
        for h in range(2):
            gather_edge(buf, g, e, h, True).wait_recv()
            for o in onward:
                gather_edge(buf, g, o, h).start()

    def gather_drain(buf, g):
        for e in range(7):
            for h in range(2):
                gather_edge(buf, g, e, h).wait_send()

    def consume_cot(blocks, first=False):
        for block in blocks:
            base = pl.multiple_of(block * width, width)

            @pl.loop(0, width // tile)
            def _(n):
                at_n = pl.multiple_of(n * tile, tile)
                term = dot(cots[block], wo[pl.ds(at_n, tile), pl.ds(base, width)], NT)
                if first:
                    acc[:, pl.ds(at_n, tile)] = term
                else:
                    acc[:, pl.ds(at_n, tile)] += term

            first = False

    def consume_rows(buf, blocks, first=False):
        for block in blocks:
            base = pl.multiple_of(block * width, width)

            @pl.loop(0, width // tile)
            def _(n):
                at_n = pl.multiple_of(n * tile, tile)
                term = dot(buf[block], wv[pl.ds(base, width), pl.ds(at_n, tile)], NN)
                if first:
                    acc[:, pl.ds(at_n, tile)] = term
                else:
                    acc[:, pl.ds(at_n, tile)] += term

            first = False

    near = [at(0, 0), at(-1, 0), at(1, 0), at(0, 1)]
    remote_blocks = [at(2, 0), at(-1, 1), at(1, 1), at(2, 1)]

    def row_sums(values, slot):
        total = values[:, 0:HD]
        for c in range(1, width // HD):
            total = total + values[:, c * HD : (c + 1) * HD]
        stat_out[pl.ds(slot, 1), :] = jnp.sum(total.T, axis=0, keepdims=True)

    def stat_copy(turn, step):
        device = (section, lax.rem(rank + step, PEERS))
        return remote(
            stat_out,
            stat_in.at[turn, step - 1],
            st_send.at[turn, step - 1],
            st_recv.at[turn, step - 1],
            device,
        )

    def stats_send(turn):
        for step in range(1, PEERS):
            stat_copy(turn, step).start()

    def stats_total(turn):
        for step in range(1, PEERS):
            stat_copy(turn, step).wait_recv()
        total = stat_out[...]
        for step in range(1, PEERS):
            total = total + stat_in[turn, step - 1]
        return (total / full).T

    load_cot.wait()
    gather_send(cots, 0, (0, 1, 2))
    load_arr.wait()
    stat_out[...] = jnp.zeros_like(stat_out)
    own = arr[...].astype(F32)
    row_sums(own, 0)
    row_sums(own * own, 1)
    gather_relay(cots, 0, 0, (3,))
    gather_relay(cots, 0, 2, (5, 6))
    send_far.wait_recv()
    keep_fet = pltpu.make_async_copy(fet, fet_ref, loc_sem.at[4])
    keep_fet.start()
    saved = jnp.where(early, fet[...].astype(F32), arr[...].astype(F32))
    row_sums(saved, 2)
    row_sums(saved * saved, 3)
    stats_send(0)
    gather_relay(cots, 0, 3, (4,))
    load_wo.wait()
    gather_wait(cots, 0, (1,))
    consume_cot(near, first=True)

    gain = gain_ref[:, pl.ds(pl.multiple_of(rank * width, width), width)]
    means = stats_total(0)
    for turn, buf in ((1, rows_b), (0, rows_f)):
        centre = means[:, 2 * turn : 2 * turn + 1]
        square = means[:, 2 * turn + 1 : 2 * turn + 2]
        inv = lax.rsqrt(square - centre * centre + EPS)
        if turn == 1:
            values = jnp.where(early, fet[...].astype(F32), arr[...].astype(F32))
        else:
            values = arr[...].astype(F32)
        unit = (values - centre) * inv
        buf[me] = (unit * gain).astype(BF16)
        if turn == 1:
            normed[...] = unit
            inv_col[...] = jnp.broadcast_to(inv, inv_col.shape)
            gather_send(rows_b, 1, (0, 1, 2))

    gather_wait(cots, 0, (4, 5, 6))
    consume_cot(remote_blocks)
    grad_ctx[...] = acc[...].astype(BF16)

    gather_relay(rows_b, 1, 0, (3,))
    gather_relay(rows_b, 1, 2, (5, 6))

    @pl.when(early)
    def _():
        gather_send(rows_f, 2, (0, 1, 2))

    gather_relay(rows_b, 1, 3, (4,))
    load_wv.wait()
    gather_wait(rows_b, 1, (1,))
    consume_rows(rows_b, near, first=True)
    gather_wait(rows_b, 1, (4, 5, 6))
    consume_rows(rows_b, remote_blocks)
    val_b[...] = acc[...].astype(BF16)

    @pl.when(early)
    def _():
        gather_relay(rows_f, 2, 0, (3,))
        gather_relay(rows_f, 2, 2, (5, 6))

    row_at = lax.broadcasted_iota(jnp.int32, (length, length), 0)
    col_at = lax.broadcasted_iota(jnp.int32, (length, length), 1)
    scale = 1.0 / math.sqrt(HD)

    def probabilities(q, v):
        scores = dot(q, v, NT) * scale
        scores = jnp.where(col_at <= row_at, scores, -jnp.inf)
        top = jnp.max(scores, axis=-1, keepdims=True)
        e = jnp.exp(scores - top)
        return e / jnp.sum(e, axis=-1, keepdims=True)

    @pl.loop(0, heads)
    def _(head):
        cols = pl.ds(pl.multiple_of(head * HD, HD), HD)
        q = rows_b[me, :, cols]
        v = val_b[:, cols]
        g = grad_ctx[:, cols]
        probs = probabilities(q, v)
        low = probs.astype(BF16)
        grad_probs = dot(g, v, NT)
        inner = jnp.sum(grad_probs * probs, axis=-1, keepdims=True)
        grad_low = (probs * (grad_probs - inner) * scale).astype(BF16)
        grad_val[:, cols] = (dot(low, g, TN) + dot(grad_low, q, TN)).astype(BF16)
        grad_q[:, cols] = dot(grad_low, v, NN)

    def reduce_edge(part, inbox, r, e, h):
        p = 1 - 2 * h
        block, device = (
            ((2, 1), (0, 1)),
            ((-p, 1), (-p, 0)),
            ((p, 1), (p, 0)),
            ((p, 0), (p, 0)),
            ((2, 0), (-p, 0)),
            ((-p, 0), (-p, 0)),
            ((0, 1), (0, 1)),
        )[e]
        mine = part.at[at(*block), pl.ds(h * half, half)]
        return remote(
            mine, inbox.at[h, e], rs_send.at[r, h, e], rs_recv.at[r, h, e], peer(*device)
        ), at(*block)

    def reduce_send(part, inbox, r, e, h):
        reduce_edge(part, inbox, r, e, h)[0].start()

    def reduce_relay(part, inbox, r, e, sources):
        for h in range(2):
            copy, block = reduce_edge(part, inbox, r, e, h)
            at_h = pl.ds(h * half, half)
            total = part[block, at_h].astype(F32)
            for s in sources:
                reduce_edge(part, inbox, r, s, h)[0].wait_recv()
                total = total + inbox[h, s].astype(F32)
            part[block, at_h] = total.astype(BF16)
            copy.start()

    def reduce_final(part, inbox, r, h):
        total = part[me, pl.ds(h * half, half)].astype(F32)
        for s in (3, 6, 5):
            reduce_edge(part, inbox, r, s, h)[0].wait_recv()
            total = total + inbox[h, s].astype(F32)
        return total

    def reduce_drain(part, inbox, r):
        for e in range(7):
            for h in range(2):
                reduce_edge(part, inbox, r, e, h)[0].wait_send()

    def reduce_leaves(part, inbox, r, term):
        term(at(2, 1))
        reduce_send(part, inbox, r, 0, 0)
        reduce_send(part, inbox, r, 0, 1)
        term(at(-1, 1))
        reduce_send(part, inbox, r, 1, 0)
        reduce_send(part, inbox, r, 2, 1)
        term(at(1, 1))
        reduce_send(part, inbox, r, 2, 0)
        reduce_send(part, inbox, r, 1, 1)
        term(at(1, 0))
        reduce_send(part, inbox, r, 3, 0)
        term(at(-1, 0))
        reduce_send(part, inbox, r, 3, 1)
        term(at(2, 0))
        term(at(0, 1))
        term(me)

    def grad_term(block):
        base = pl.multiple_of(block * width, width)

        @pl.loop(0, width // tile)
        def _(n):
            at_n = pl.multiple_of(n * tile, tile)
            row_n = pl.multiple_of(base + at_n, tile)
            term = dot(grad_val[...], wv[pl.ds(row_n, tile), :], NT)
            part_g[block, :, pl.ds(at_n, tile)] = term.astype(BF16)

    def grad_term_own(block):
        base = pl.multiple_of(block * width, width)

        @pl.loop(0, width // tile)
        def _(n):
            at_n = pl.multiple_of(n * tile, tile)
            row_n = pl.multiple_of(base + at_n, tile)
            term = dot(grad_val[...], wv[pl.ds(row_n, tile), :], NT)
            term = term + grad_q[:, pl.ds(at_n, tile)]
            part_g[block, :, pl.ds(at_n, tile)] = term.astype(BF16)

    def head_term(block):
        base = pl.multiple_of(block * width, width)

        @pl.loop(0, width // tile)
        def _(n):
            at_n = pl.multiple_of(n * tile, tile)
            col_n = pl.multiple_of(base + at_n, tile)
            term = dot(ctx[...], wo[:, pl.ds(col_n, tile)], NN)
            part_h[block, :, pl.ds(at_n, tile)] = term.astype(BF16)

    reduce_leaves(
        part_g, in_g, 0, lambda block: grad_term_own(block) if block is me else grad_term(block)
    )

    @pl.when(early)
    def _():
        gather_relay(rows_f, 2, 3, (4,))
        gather_wait(rows_f, 2, (1,))
        consume_rows(rows_f, near, first=True)

    reduce_relay(part_g, in_g, 0, 4, (0,))
    reduce_relay(part_g, in_g, 0, 6, (1, 2))

    @pl.when(early)
    def _():
        gather_wait(rows_f, 2, (4, 5, 6))
        consume_rows(rows_f, remote_blocks)
        val_f[...] = acc[...].astype(BF16)

    @pl.when(jnp.logical_not(early))
    def _():
        val_f[...] = val_b[...]

    reduce_relay(part_g, in_g, 0, 5, (4,))

    @pl.loop(0, heads)
    def _(head):
        cols = pl.ds(pl.multiple_of(head * HD, HD), HD)
        v = val_f[:, cols]
        low = probabilities(rows_f[me, :, cols], v).astype(BF16)
        ctx[:, cols] = dot(low, v, NN).astype(BF16)

    reduce_leaves(part_h, in_h, 1, head_term)

    for h in range(2):
        at_h = pl.ds(h * half, half)
        acc[at_h, :] = reduce_final(part_g, in_g, 0, h)
    grads = acc[...]
    unit = normed[...]
    gg_ref[...] = jnp.sum(grads * unit, axis=0, keepdims=True)
    grad_unit = grads * gain
    for step in range(1, PEERS):
        stat_copy(0, step).wait_send()
    row_sums(grad_unit, 0)
    row_sums(grad_unit * unit, 1)
    stats_send(1)
    reduce_relay(part_h, in_h, 1, 4, (0,))
    reduce_relay(part_h, in_h, 1, 6, (1, 2))
    means = stats_total(1)
    dx = cots[me].astype(F32) + inv_col[:, 0:1] * (
        acc[...] * gain - means[:, 0:1] - normed[...] * means[:, 1:2]
    )
    dx_buf[...] = dx.astype(BF16)
    send_dx = remote(dx_buf, ret_ref, far_send.at[1], far_recv.at[1], prev_section)
    send_dx.start()
    reduce_relay(part_h, in_h, 1, 5, (4,))
    send_y = []
    for h in range(2):
        at_h = pl.ds(h * half, half)
        y_buf[at_h, :] = (arr[at_h, :].astype(F32) + reduce_final(part_h, in_h, 1, h)).astype(BF16)
        copy = remote(
            y_buf.at[at_h], fwd_ref.at[at_h], far_send.at[2 + h], far_recv.at[2 + h], next_section
        )
        copy.start()
        send_y.append(copy)

    gather_drain(cots, 0)
    gather_drain(rows_b, 1)

    @pl.when(early)
    def _():
        gather_drain(rows_f, 2)

    reduce_drain(part_g, in_g, 0)
    reduce_drain(part_h, in_h, 1)
    for step in range(1, PEERS):
        stat_copy(1, step).wait_send()
    send_far.wait_send()
    keep_fet.wait()
    send_dx.wait()
    for copy in send_y:
        copy.wait()


def body(arriving, cotangent, evicted, ln_gain, value_weight, out_weight, fetch_slot):
    sections = lax.axis_size("section")
    position = lax.axis_index("section")
    length, width = arriving.shape[1:]
    full = PEERS * width
    send_slot = fetch_slot[sections - 1 - position]
    outgoing = lax.dynamic_index_in_dim(evicted[0], send_slot, 0, keepdims=False)
    half = length // 2
    anywhere = pl.BlockSpec(memory_space=pl.ANY)
    in_vmem = pl.BlockSpec(memory_space=pltpu.VMEM)
    rows = jax.ShapeDtypeStruct((length, width), BF16)
    dma = pltpu.SemaphoreType.DMA
    forwarded, returned, fetched, gain_grad = pl.pallas_call(
        functools.partial(kernel, sections),
        out_shape=(rows, rows, rows, jax.ShapeDtypeStruct((1, width), F32)),
        in_specs=[anywhere, anywhere, anywhere, in_vmem, anywhere, anywhere],
        out_specs=(anywhere, anywhere, anywhere, in_vmem),
        scratch_shapes=[
            pltpu.VMEM((full, width), BF16),
            pltpu.VMEM((width, full), BF16),
            pltpu.VMEM((PEERS, length, width), BF16),
            pltpu.VMEM((PEERS, length, width), BF16),
            pltpu.VMEM((PEERS, length, width), BF16),
            pltpu.VMEM((PEERS, length, width), BF16),
            pltpu.VMEM((PEERS, length, width), BF16),
            pltpu.VMEM((2, 7, half, width), BF16),
            pltpu.VMEM((2, 7, half, width), BF16),
            pltpu.VMEM((length, width), F32),
            pltpu.VMEM((length, width), BF16),
            pltpu.VMEM((length, width), BF16),
            pltpu.VMEM((length, width), BF16),
            pltpu.VMEM((length, width), BF16),
            pltpu.VMEM((length, width), F32),
            pltpu.VMEM((length, width), BF16),
            pltpu.VMEM((length, width), BF16),
            pltpu.VMEM((length, width), BF16),
            pltpu.VMEM((length, width), F32),
            pltpu.VMEM((length, HD), F32),
            pltpu.VMEM((8, length), F32),
            pltpu.VMEM((2, PEERS - 1, 8, length), F32),
            pltpu.VMEM((length, width), BF16),
            pltpu.VMEM((length, width), BF16),
            dma((5,)),
            dma((3, 2, 7)),
            dma((3, 2, 7)),
            dma((2, 2, 7)),
            dma((2, 2, 7)),
            dma((2, PEERS - 1)),
            dma((2, PEERS - 1)),
            dma((4,)),
            dma((4,)),
        ],
        compiler_params=pltpu.CompilerParams(
            collective_id=0, has_side_effects=True, vmem_limit_bytes=60 * 1024 * 1024
        ),
    )(arriving[0], cotangent[0], outgoing, ln_gain, value_weight[0], out_weight[0])
    return (forwarded[None], returned[None], gain_grad, fetched[None])


def solution(mesh):
    return jax.shard_map(
        body,
        mesh=mesh,
        in_specs=(
            P("section", None, "tp"),
            P("section", None, "tp"),
            P("section", None, None, "tp"),
            P("section", None),
            P("section", None, "tp"),
            P("section", "tp", None),
            P(),
        ),
        out_specs=(
            P("section", None, "tp"),
            P("section", None, "tp"),
            P("section", "tp"),
            P("section", None, "tp"),
        ),
        check_vma=False,
    )
```

time: 554 us -> 146 us (0.26)
  the two profiles are of different devices: /device:TPU:96 before, /device:TPU:1 now
where the time goes in v2:
time: 146 us; the launch traced here: 145 us
  Pallas kernels  134 us (92%)
  local copies, waits for them, and re-layouts  8.65 us (6%)
  between operations  2.61 us (2%)
    pallas_call x1, Pallas kernels, body(): pl.pallas_call(functools.partial(kernel, sections), out_shape=(rows, rows...  134 us
    unnamed x6, local copies, waits for them, and re-layouts  6.56 us

profile of v2, /device:TPU:1, one launch (start us, length us, event | category | flops | bytes accessed | tf_op | source)
XLA Modules:
  0.0 145.2 jit_solution(9056196607934891096)
XLA Ops:
  0.6 0.0 copy-start
  0.7 1.3 dynamic_slice.7
  3.9 0.0 copy-done
  3.9 0.8 dynamic-slice_bitcast_fusion.out_ref
  4.7 133.9 %shard_map.102 = (bf16[256,768]{1,0:T(8,128)(2,1)}, bf16[256,768]{1,0:T(8,128)(2,1)}, bf16[256,768]{1,0:T(8,128)(2,1)}, f32[1,768]{1,0:T(1,128)}) custom-call(bf16[256,768]{1,0:T(8,128)(2,1)} %bitcast.15, bf16[256,768]{1,0:T(8,128)(2,1)} %bitcast.16, bf16[256,768]{1,0:T(8,128)(2,1)} %dynamic-slice_bitcast_fusion.out_ref, f32[1,6144]{1,0:T(1,128)} %gain_ref.1, ...), custom_call_target="tpu_custom_call" | custom-call | tf_op jit(solution)/shard_map/pallas_call | solution.py:496
  138.6 1.8 %copy.15 = bf16[1,256,768]{2,1,0:T(8,128)(2,1)} copy(bf16[1,256,768]{2,1,0:T(8,128)(2,1)} %bitcast.14) | data formatting | bytes 786432
  140.4 1.8 %copy.16 = bf16[1,256,768]{2,1,0:T(8,128)(2,1)} copy(bf16[1,256,768]{2,1,0:T(8,128)(2,1)} %bitcast.13) | data formatting | bytes 786432
  142.2 1.2 copy.17
  143.4 1.8 %copy.18 = bf16[1,256,768]{2,1,0:T(8,128)(2,1)} copy(bf16[1,256,768]{2,1,0:T(8,128)(2,1)} %bitcast.12) | data formatting | bytes 786432
Async XLA Ops:
  0.6 3.3 %copy-start = (bf16[1,2,256,768]{3,2,1,0:T(8,128)(2,1)S(1)}, bf16[1,2,256,768]{3,2,1,0:T(8,128)(2,1)}, u32[]{:S(2)}) copy-start(bf16[1,2,256,768]{3,2,1,0:T(8,128)(2,1)} %param.9) | copy-start | bytes 2359300

commit v3 on v2

v3 whole, which is shorter than its diff:
```python
import functools
import math

import jax
import jax.numpy as jnp
from jax import lax
from jax.experimental import pallas as pl
from jax.experimental.pallas import tpu as pltpu
from jax.sharding import PartitionSpec as P

HD = 128
EPS = 1e-05
RING = 4
PEERS = 8
MESH = pl.DeviceIdType.MESH
BF16 = jnp.bfloat16
F32 = jnp.float32
NT = (((1,), (1,)), ((), ()))
NN = (((1,), (0,)), ((), ()))
TN = (((0,), (0,)), ((), ()))
OWNER = (0, 0)
TREE_X = (
    (OWNER, (1, 0)),
    (OWNER, (-1, 0)),
    (OWNER, (0, 1)),
    ((1, 0), (2, 0)),
    ((2, 0), (2, 1)),
    ((0, 1), (1, 1)),
    ((0, 1), (-1, 1)),
)
TREE_Z = (
    (OWNER, (1, 0)),
    (OWNER, (-1, 0)),
    (OWNER, (0, 1)),
    ((1, 0), (2, 0)),
    ((1, 0), (1, 1)),
    ((2, 0), (2, 1)),
    ((0, 1), (-1, 1)),
)
EDGES = len(TREE_X)
BLOCKS = (OWNER, (-1, 0), (1, 0), (0, 1), (2, 0), (-1, 1), (1, 1), (2, 1))


def children(tree, node):
    return [e for e, (a, _) in enumerate(tree) if a == node]


def depth(tree, e):
    a = tree[e][0]
    return 1 if a == OWNER else 1 + max(depth(tree, k) for k, (_, b) in enumerate(tree) if b == a)


def height(tree, e):
    below = children(tree, tree[e][1])
    return 1 + max(height(tree, k) for k in below) if below else 0


def two_chunks(first, count):
    half = count // 2
    return ((TREE_X, 1, first, half), (TREE_X, -1, first + half, half))


def three_chunks(count):
    side = max(16, count * 5 // 16 // 16 * 16)
    return (
        (TREE_X, 1, 0, side),
        (TREE_X, -1, side, side),
        (TREE_Z, 1, 2 * side, count - 2 * side),
    )


def dot(a, b, dims):
    return lax.dot_general(a, b, dims, preferred_element_type=F32)


def kernel(
    sections,
    arr_ref,
    cot_ref,
    ev_ref,
    slot_ref,
    gain_ref,
    wv_ref,
    wo_ref,
    fwd_ref,
    ret_ref,
    fet_ref,
    gg_ref,
    wv,
    wo,
    cots,
    rows_b,
    rows_f,
    part_g,
    part_h,
    in_g,
    in_h,
    acc,
    grad_ctx,
    val_b,
    val_f,
    grad_val,
    grad_q,
    ctx,
    arr,
    stored,
    outgoing,
    fet,
    far_rows,
    query,
    normed,
    inv_col,
    stat_out,
    stat_in,
    totals,
    far_totals,
    y_buf,
    dx_buf,
    loc_sem,
    ag_send,
    ag_recv,
    rs_send,
    rs_recv,
    st_send,
    st_recv,
    far_send,
    far_recv,
    help_send,
    help_recv,
):
    length, width = arr.shape
    half = length // 2
    helped = half
    chunks = two_chunks(0, length)
    whole = three_chunks(length)
    tables = (whole, whole, two_chunks(helped, length - helped), two_chunks(0, helped))
    heads = width // HD
    full = PEERS * width
    tile = min(256, width)
    section = lax.axis_index("section")
    rank = lax.axis_index("tp")
    x = rank % RING
    z = rank // RING
    early = section < sections // 2
    late = section >= sections // 2

    def at(dx, dz):
        return lax.rem(z + dz, 2) * RING + lax.rem(x + dx + RING, RING)

    def peer(dx, dz):
        return (section, at(dx, dz))

    def remote(src, dst, ssem, rsem, device):
        return pltpu.make_async_remote_copy(
            src_ref=src,
            dst_ref=dst,
            send_sem=ssem,
            recv_sem=rsem,
            device_id=device,
            device_id_type=MESH,
        )

    me = at(0, 0)
    next_section = (lax.rem(section + 1, sections), rank)
    prev_section = (lax.rem(section + sections - 1, sections), rank)
    mirror = (sections - 1 - section, rank)
    helper = (sections - 1 - section, at(0, 1))

    load_cot = pltpu.make_async_copy(cot_ref, cots.at[me], loc_sem.at[0])
    load_arr = pltpu.make_async_copy(arr_ref, arr, loc_sem.at[1])
    load_wo = pltpu.make_async_copy(wo_ref, wo, loc_sem.at[2])
    load_wv = pltpu.make_async_copy(wv_ref, wv, loc_sem.at[3])
    load_evicted = pltpu.make_async_copy(ev_ref, stored, loc_sem.at[5])
    load_evicted.start()
    load_cot.start()
    load_arr.start()

    barrier = pltpu.get_barrier_semaphore()
    for step in range(1, PEERS):
        pl.semaphore_signal(
            barrier, inc=1, device_id=(section, lax.rem(rank + step, PEERS)), device_id_type=MESH
        )
    for device in (next_section, prev_section, mirror, helper):
        pl.semaphore_signal(barrier, inc=1, device_id=device, device_id_type=MESH)
    pl.semaphore_wait(barrier, PEERS + 3)

    def gather_edge(buf, g, c, e, landing=False):
        tree, p, first, count = tables[g][c]
        a, b = tree[e]
        dx, dz = b if landing else a
        rows = buf.at[at(-dx * p, dz), pl.ds(first, count)]
        device = peer((b[0] - a[0]) * p, (b[1] - a[1]) % 2)
        return remote(rows, rows, ag_send.at[g, c, e], ag_recv.at[g, c, e], device)

    def gather_roots(buf, g):
        for e in range(3):
            for c in range(len(tables[g])):
                gather_edge(buf, g, c, e).start()

    def gather_relay(buf, g, level):
        for e in (0, 2, 1, 3, 4, 5, 6):
            for c, (tree, *_) in enumerate(tables[g]):
                onward = children(tree, tree[e][1])
                if depth(tree, e) == level and onward:
                    gather_edge(buf, g, c, e, True).wait_recv()
                    for o in onward:
                        gather_edge(buf, g, c, o).start()

    def gather_wait(buf, g, near_only):
        for e in range(EDGES):
            for c, (tree, *_) in enumerate(tables[g]):
                leaf = not children(tree, tree[e][1])
                if leaf and (depth(tree, e) == 1) == near_only:
                    gather_edge(buf, g, c, e, True).wait_recv()

    def gather_drain(buf, g):
        for e in range(EDGES):
            for c in range(len(tables[g])):
                gather_edge(buf, g, c, e).wait_send()

    def help_copy(j, landing=False):
        dx, dz = BLOCKS[j]
        block = at(dx, (dz + 1) % 2) if landing else at(dx, dz)
        return remote(
            rows_b.at[block, pl.ds(0, helped)],
            far_rows.at[block],
            help_send.at[j],
            help_recv.at[j],
            helper,
        )

    def consume_cot(blocks, first=False):
        for block in blocks:
            base = pl.multiple_of(block * width, width)

            @pl.loop(0, width // tile)
            def _(n):
                at_n = pl.multiple_of(n * tile, tile)
                term = dot(cots[block], wo[pl.ds(at_n, tile), pl.ds(base, width)], NT)
                if first:
                    acc[:, pl.ds(at_n, tile)] = term
                else:
                    acc[:, pl.ds(at_n, tile)] += term

            first = False

    def consume_rows(buf, blocks, first=False):
        for block in blocks:
            base = pl.multiple_of(block * width, width)

            @pl.loop(0, width // tile)
            def _(n):
                at_n = pl.multiple_of(n * tile, tile)
                term = dot(buf[block], wv[pl.ds(base, width), pl.ds(at_n, tile)], NN)
                if first:
                    acc[:, pl.ds(at_n, tile)] = term
                else:
                    acc[:, pl.ds(at_n, tile)] += term

            first = False

    blocks = [at(*rel) for rel in BLOCKS]
    near, remote_blocks = blocks[:4], blocks[4:]

    def row_sums(values, turn, row):
        total = values[:, 0:HD]
        for c in range(1, heads):
            total = total + values[:, c * HD : (c + 1) * HD]
        sums = jnp.sum(total.T, axis=0, keepdims=True)
        stat_out[turn, pl.ds(row, 1), pl.ds(0, values.shape[0])] = sums

    def stat_copy(turn, step):
        device = (section, lax.rem(rank + step, PEERS))
        return remote(
            stat_out.at[turn],
            stat_in.at[turn, step - 1],
            st_send.at[turn, step - 1],
            st_recv.at[turn, step - 1],
            device,
        )

    def stats_send(turn):
        for step in range(1, PEERS):
            stat_copy(turn, step).start()

    def stats_total(turn):
        total = stat_out[turn]
        for step in range(1, PEERS):
            stat_copy(turn, step).wait_recv()
            total = total + stat_in[turn, step - 1]
        return total / full

    row_at = lax.broadcasted_iota(jnp.int32, (length, length), 0)
    col_at = lax.broadcasted_iota(jnp.int32, (length, length), 1)
    scale = 1.0 / math.sqrt(HD)

    def probabilities(q, v):
        scores = dot(q, v, NT) * scale
        scores = jnp.where(col_at <= row_at, scores, -jnp.inf)
        top = jnp.max(scores, axis=-1, keepdims=True)
        e = jnp.exp(scores - top)
        return e / jnp.sum(e, axis=-1, keepdims=True)

    def reduce_edge(part, inbox, r, c, e):
        tree, p, first, count = chunks[c]
        a, b = tree[e]
        return remote(
            part.at[at(-b[0] * p, b[1]), pl.ds(first, count)],
            inbox.at[e, pl.ds(first, count)],
            rs_send.at[r, c, e],
            rs_recv.at[r, c, e],
            peer((a[0] - b[0]) * p, (a[1] - b[1]) % 2),
        )

    def reduce_leaves(part, inbox, r, term):
        for block in ((2, 1), (-1, 1), (1, 1), (1, 0), (-1, 0), (2, 0), (0, 1), OWNER):
            term(block)
            for c, (tree, p, *_) in enumerate(chunks):
                for e, (_, b) in enumerate(tree):
                    same = ((-b[0] * p) % RING, b[1]) == (block[0] % RING, block[1])
                    if same and height(tree, e) == 0:
                        reduce_edge(part, inbox, r, c, e).start()

    def reduce_relay(part, inbox, r, level):
        for e in (3, 2, 1, 0, 4, 5, 6):
            for c, (tree, p, first, count) in enumerate(chunks):
                if height(tree, e) != level:
                    continue
                b = tree[e][1]
                block, rows = at(-b[0] * p, b[1]), pl.ds(first, count)
                total = part[block, rows].astype(F32)
                for k in children(tree, b):
                    reduce_edge(part, inbox, r, c, k).wait_recv()
                    total = total + inbox[k, rows].astype(F32)
                part[block, rows] = total.astype(BF16)
                reduce_edge(part, inbox, r, c, e).start()

    def reduce_final(part, inbox, r, c):
        _, _, first, count = chunks[c]
        rows = pl.ds(first, count)
        total = part[me, rows].astype(F32)
        for k in (1, 2, 0):
            reduce_edge(part, inbox, r, c, k).wait_recv()
            total = total + inbox[k, rows].astype(F32)
        return rows, total

    def reduce_drain(part, inbox, r):
        for e in range(EDGES):
            for c in range(len(chunks)):
                reduce_edge(part, inbox, r, c, e).wait_send()

    def grad_term(rel):
        block = at(*rel)
        base = pl.multiple_of(block * width, width)

        @pl.loop(0, width // tile)
        def _(n):
            at_n = pl.multiple_of(n * tile, tile)
            row_n = pl.multiple_of(base + at_n, tile)
            term = dot(grad_val[...], wv[pl.ds(row_n, tile), :], NT)
            if rel == OWNER:
                term = term + grad_q[:, pl.ds(at_n, tile)]
            part_g[block, :, pl.ds(at_n, tile)] = term.astype(BF16)

    def head_term(rel):
        block = at(*rel)
        base = pl.multiple_of(block * width, width)

        @pl.loop(0, width // tile)
        def _(n):
            at_n = pl.multiple_of(n * tile, tile)
            col_n = pl.multiple_of(base + at_n, tile)
            term = dot(ctx[...], wo[:, pl.ds(col_n, tile)], NN)
            part_h[block, :, pl.ds(at_n, tile)] = term.astype(BF16)

    gain = gain_ref[:, pl.ds(pl.multiple_of(rank * width, width), width)]
    top, bottom = pl.ds(0, helped), pl.ds(helped, length - helped)

    def normalise(values, centre, inv, rows):
        unit = (values.astype(F32) - centre) * inv
        normed[rows, :] = unit
        inv_col[rows, :] = jnp.broadcast_to(inv, (unit.shape[0], HD))
        return (unit * gain).astype(BF16)

    def centre_and_inv(means):
        centre = means[:, 0:1]
        return centre, lax.rsqrt(means[:, 1:2] - centre * centre + EPS)

    def send_totals():
        return remote(totals, far_totals, far_send.at[6], far_recv.at[6], mirror)

    def far_half(k, rows):
        return remote(outgoing.at[rows], fet.at[rows], far_send.at[k], far_recv.at[k], mirror)

    def helped_rows():
        for j in range(PEERS):
            help_copy(j, True).wait_recv()
        pltpu.make_async_copy(far_rows.at[me], fet_ref.at[top], loc_sem.at[5]).start()
        total = jnp.zeros((helped, HD), F32)
        squares = jnp.zeros((helped, HD), F32)
        for block in range(PEERS):
            for c in range(heads):
                part = far_rows[block, :, c * HD : (c + 1) * HD].astype(F32)
                total = total + part
                squares = squares + part * part
        centre = jnp.sum(total, axis=-1, keepdims=True) / full
        square = jnp.sum(squares, axis=-1, keepdims=True) / full
        inv = lax.rsqrt(square - centre * centre + EPS)
        for block in range(PEERS):
            unit = (far_rows[block].astype(F32) - centre) * inv
            gain_block = gain_ref[:, block * width : (block + 1) * width]
            rows_b[block, top] = (unit * gain_block).astype(BF16)
        normalise(far_rows[me], centre, inv, top)

    load_evicted.wait()
    outgoing[...] = jnp.where(slot_ref[sections - 1 - section] == 0, stored[0], stored[1])

    @pl.when(late)
    def _():
        rows_b[me, top] = outgoing[top, :]
        gather_roots(rows_b, 3)
        help_copy(0).start()

    load_arr.wait()
    stat_out[...] = jnp.zeros_like(stat_out)
    own = arr[...].astype(F32)
    row_sums(own, 0, 0)
    row_sums(own * own, 0, 1)
    away = outgoing[...].astype(F32)
    row_sums(away, 0, 2)
    row_sums(away * away, 0, 3)
    stats_send(0)
    load_cot.wait()

    @pl.when(early)
    def _():
        gather_roots(cots, 0)

    load_wv.start()
    load_wo.start()

    @pl.when(late)
    def _():
        gather_relay(rows_b, 3, 1)
        gather_wait(rows_b, 3, True)
        for j in range(1, 4):
            help_copy(j).start()
        gather_relay(rows_b, 3, 2)

    means = stats_total(0)
    totals[...] = means
    rows_f[me] = normalise(arr[...], *centre_and_inv(means.T), pl.ds(0, length))
    gather_roots(rows_f, 1)
    send_totals().start()
    far_half(0, bottom).start()
    gather_relay(rows_f, 1, 1)
    send_totals().wait_recv()
    far_half(0, bottom).wait_recv()
    keep_bottom = pltpu.make_async_copy(fet.at[bottom], fet_ref.at[bottom], loc_sem.at[4])
    keep_bottom.start()

    @pl.when(early)
    def _():
        far_means = far_totals[...].T[helped:, 2:4]
        rows_b[me, bottom] = normalise(fet[bottom, :], *centre_and_inv(far_means), bottom)

    @pl.when(late)
    def _():
        gather_roots(cots, 0)
        gather_wait(rows_b, 3, False)
        for j in range(4, 8):
            help_copy(j).start()

    gather_relay(rows_f, 1, 2)

    @pl.when(early)
    def _():
        gather_roots(rows_b, 2)
        far_half(1, top).start()

    load_wv.wait()
    gather_wait(rows_f, 1, True)
    consume_rows(rows_f, near, first=True)
    gather_relay(cots, 0, 1)

    @pl.when(early)
    def _():
        gather_relay(rows_b, 2, 1)

    gather_wait(rows_f, 1, False)
    consume_rows(rows_f, remote_blocks)
    val_f[...] = acc[...].astype(BF16)
    load_wo.wait()
    gather_wait(cots, 0, True)
    consume_cot(near, first=True)
    gather_relay(cots, 0, 2)

    @pl.loop(0, heads)
    def _(head):
        cols = pl.ds(pl.multiple_of(head * HD, HD), HD)
        v = val_f[:, cols]
        low = probabilities(rows_f[me, :, cols], v).astype(BF16)
        ctx[:, cols] = dot(low, v, NN).astype(BF16)

    @pl.when(early)
    def _():
        gather_relay(rows_b, 2, 2)

    reduce_leaves(part_h, in_h, 0, head_term)

    @pl.when(early)
    def _():
        helped_rows()

    gather_wait(cots, 0, False)
    consume_cot(remote_blocks)
    grad_ctx[...] = acc[...].astype(BF16)

    @pl.when(early)
    def _():
        gather_wait(rows_b, 2, True)
        gather_wait(rows_b, 2, False)
        consume_rows(rows_b, blocks, first=True)
        val_b[...] = acc[...].astype(BF16)
        query[...] = rows_b[me]

    @pl.when(late)
    def _():
        far_half(1, top).wait_recv()
        pltpu.make_async_copy(fet.at[top], fet_ref.at[top], loc_sem.at[5]).start()
        val_b[...] = val_f[...]
        query[...] = rows_f[me]

    @pl.loop(0, heads)
    def _(head):
        cols = pl.ds(pl.multiple_of(head * HD, HD), HD)
        q = query[:, cols]
        v = val_b[:, cols]
        g = grad_ctx[:, cols]
        probs = probabilities(q, v)
        low = probs.astype(BF16)
        grad_probs = dot(g, v, NT)
        inner = jnp.sum(grad_probs * probs, axis=-1, keepdims=True)
        grad_low = (probs * (grad_probs - inner) * scale).astype(BF16)
        grad_val[:, cols] = (dot(low, g, TN) + dot(grad_low, q, TN)).astype(BF16)
        grad_q[:, cols] = dot(grad_low, v, NN)

    reduce_leaves(part_g, in_g, 1, grad_term)

    def gradient_sums(scaled):
        first = jnp.zeros((length, HD), F32)
        second = jnp.zeros((length, HD), F32)
        for block in range(PEERS):
            for c in range(heads):
                cols = slice(c * HD, (c + 1) * HD)
                term = part_g[block, :, cols].astype(F32)
                gain_cols = slice(block * width + c * HD, block * width + (c + 1) * HD)
                first = first + term * gain_ref[:, gain_cols]
                second = second + term * scaled[block, :, cols].astype(F32)
        stat_out[1, 0:1, :] = jnp.sum(first.T, axis=0, keepdims=True)
        stat_out[1, 1:2, :] = jnp.sum(second.T, axis=0, keepdims=True)

    @pl.when(early)
    def _():
        gradient_sums(rows_b)

    @pl.when(late)
    def _():
        gradient_sums(rows_f)

    stats_send(1)
    reduce_relay(part_g, in_g, 1, 1)
    reduce_relay(part_h, in_h, 0, 1)
    reduce_relay(part_g, in_g, 1, 2)
    reduce_relay(part_h, in_h, 0, 2)
    means = stats_total(1).T
    gain_sum = jnp.zeros((1, width), F32)
    shifts = []
    for c in range(len(chunks)):
        rows, grads = reduce_final(part_g, in_g, 1, c)
        unit = normed[rows, :]
        dx = cots[me, rows].astype(F32) + inv_col[rows, 0:1] * (
            grads * gain
            - means[c * half : (c + 1) * half, 0:1]
            - unit * means[c * half : (c + 1) * half, 1:2]
        )
        dx_buf[rows, :] = dx.astype(BF16)
        copy = remote(
            dx_buf.at[rows], ret_ref.at[rows], far_send.at[2 + c], far_recv.at[2 + c], prev_section
        )
        copy.start()
        shifts.append(copy)
        gain_sum = gain_sum + jnp.sum(grads * unit, axis=0, keepdims=True)
    for c in range(len(chunks)):
        rows, total = reduce_final(part_h, in_h, 0, c)
        y_buf[rows, :] = (arr[rows, :].astype(F32) + total).astype(BF16)
        copy = remote(
            y_buf.at[rows], fwd_ref.at[rows], far_send.at[4 + c], far_recv.at[4 + c], next_section
        )
        copy.start()
        shifts.append(copy)
    gg_ref[...] = gain_sum

    gather_drain(cots, 0)
    gather_drain(rows_f, 1)
    for step in range(1, PEERS):
        stat_copy(0, step).wait_send()
        stat_copy(1, step).wait_send()

    @pl.when(early)
    def _():
        gather_drain(rows_b, 2)
        far_half(1, top).wait_send()
        pltpu.make_async_copy(far_rows.at[me], fet_ref.at[top], loc_sem.at[5]).wait()

    @pl.when(late)
    def _():
        gather_drain(rows_b, 3)
        for j in range(PEERS):
            help_copy(j).wait_send()
        pltpu.make_async_copy(fet.at[top], fet_ref.at[top], loc_sem.at[5]).wait()

    reduce_drain(part_g, in_g, 1)
    reduce_drain(part_h, in_h, 0)
    far_half(0, bottom).wait_send()
    keep_bottom.wait()
    send_totals().wait_send()
    for copy in shifts:
        copy.wait()


def publish(*refs):
    landed, results, held, sems = refs[:4], refs[4:8], refs[8:12], refs[12]
    inward = [pltpu.make_async_copy(landed[i], held[i], sems.at[0, i]) for i in range(4)]
    outward = [pltpu.make_async_copy(held[i], results[i], sems.at[1, i]) for i in range(4)]
    for copy in inward:
        copy.start()
    for i in range(4):
        inward[i].wait()
        outward[i].start()
    for copy in outward:
        copy.wait()


def body(arriving, cotangent, evicted, ln_gain, value_weight, out_weight, fetch_slot):
    sections = lax.axis_size("section")
    length, width = arriving.shape[1:]
    full = PEERS * width
    anywhere = pl.BlockSpec(memory_space=pl.ANY)
    in_vmem = pl.BlockSpec(memory_space=pltpu.VMEM)
    in_smem = pl.BlockSpec(memory_space=pltpu.SMEM)
    rows = jax.ShapeDtypeStruct((length, width), BF16)
    dma = pltpu.SemaphoreType.DMA
    gathered = pltpu.VMEM((PEERS, length, width), BF16)
    inbox = pltpu.VMEM((EDGES, length, width), BF16)
    share = pltpu.VMEM((length, width), BF16)
    wide = pltpu.VMEM((length, width), F32)
    out_shape = (rows, rows, rows, jax.ShapeDtypeStruct((1, width), F32))
    landed = pl.pallas_call(
        functools.partial(kernel, sections),
        out_shape=out_shape,
        in_specs=[anywhere, anywhere, anywhere, in_smem, in_vmem, anywhere, anywhere],
        out_specs=(anywhere, anywhere, anywhere, in_vmem),
        scratch_shapes=[
            pltpu.VMEM((full, width), BF16),
            pltpu.VMEM((width, full), BF16),
            gathered,
            gathered,
            gathered,
            gathered,
            gathered,
            inbox,
            inbox,
            wide,
            share,
            share,
            share,
            share,
            wide,
            share,
            share,
            pltpu.VMEM((2, length, width), BF16),
            share,
            share,
            pltpu.VMEM((PEERS, length // 2, width), BF16),
            share,
            wide,
            pltpu.VMEM((length, HD), F32),
            pltpu.VMEM((2, 8, length), F32),
            pltpu.VMEM((2, PEERS - 1, 8, length), F32),
            pltpu.VMEM((8, length), F32),
            pltpu.VMEM((8, length), F32),
            share,
            share,
            dma((6,)),
            dma((4, 3, EDGES)),
            dma((4, 3, EDGES)),
            dma((2, 2, EDGES)),
            dma((2, 2, EDGES)),
            dma((2, PEERS - 1)),
            dma((2, PEERS - 1)),
            dma((7,)),
            dma((7,)),
            dma((PEERS,)),
            dma((PEERS,)),
        ],
        compiler_params=pltpu.CompilerParams(
            collective_id=0, has_side_effects=True, vmem_limit_bytes=60 * 1024 * 1024
        ),
    )(arriving[0], cotangent[0], evicted[0], fetch_slot, ln_gain, value_weight[0], out_weight[0])
    forwarded, returned, fetched, gain_grad = pl.pallas_call(
        publish,
        out_shape=out_shape,
        in_specs=[anywhere] * 4,
        out_specs=(anywhere,) * 4,
        scratch_shapes=[share, share, share, pltpu.VMEM((1, width), F32), dma((2, 4))],
        compiler_params=pltpu.CompilerParams(vmem_limit_bytes=60 * 1024 * 1024),
    )(*landed)
    return (forwarded[None], returned[None], gain_grad, fetched[None])


def solution(mesh):
    return jax.shard_map(
        body,
        mesh=mesh,
        in_specs=(
            P("section", None, "tp"),
            P("section", None, "tp"),
            P("section", None, None, "tp"),
            P("section", None),
            P("section", None, "tp"),
            P("section", "tp", None),
            P(),
        ),
        out_specs=(
            P("section", None, "tp"),
            P("section", None, "tp"),
            P("section", "tp"),
            P("section", None, "tp"),
        ),
        check_vma=False,
    )
```

time: 146 us -> 133 us (0.911)
  the two profiles are of different devices: /device:TPU:1 before, /device:TPU:96 now
where the time goes in v3:
time: 133 us
  Pallas kernels  132 us (99%)
    pallas_call x1, Pallas kernels, body(): pl.pallas_call(functools.partial(kernel, sections), out_shape=out_shape,...  130 us

profile of v3, /device:TPU:96, one launch (start us, length us, event | category | flops | bytes accessed | tf_op | source)
XLA Modules:
  0.0 133.1 jit_solution(5269570310610290827)
XLA Ops:
  0.6 130.2 %shard_map.102 = (bf16[256,768]{1,0:T(8,128)(2,1)}, bf16[256,768]{1,0:T(8,128)(2,1)}, bf16[256,768]{1,0:T(8,128)(2,1)}, f32[1,768]{1,0:T(1,128)}) custom-call(bf16[256,768]{1,0:T(8,128)(2,1)} %bitcast.11, bf16[256,768]{1,0:T(8,128)(2,1)} %bitcast.12, bf16[2,256,768]{2,1,0:T(8,128)(2,1)} %bitcast.10, s32[16]{0:T(128)} %slot_ref.1, f32[1,6144]{1,0:T(1,128)} %gain_ref.1, ...), custom_call_target="tpu_custom_call" | custom-call | tf_op jit(solution)/shard_map/pallas_call | solution.py:659
  130.9 2.1 %shard_map.103 = (bf16[256,768]{1,0:T(8,128)(2,1)}, bf16[256,768]{1,0:T(8,128)(2,1)}, bf16[256,768]{1,0:T(8,128)(2,1)}, f32[1,768]{1,0:T(1,128)}) custom-call(bf16[256,768]{1,0:T(8,128)(2,1)} %get-tuple-element.12.refs_0_, bf16[256,768]{1,0:T(8,128)(2,1)} %get-tuple-element.13.refs_1_, bf16[256,768]{1,0:T(8,128)(2,1)} %get-tuple-element.14.refs_2_, ...), custom_call_target="tpu_custom_call" | custom-call | tf_op jit(solution)/shard_map/pallas_call | solution.py:711

commit v4 on v3

--- a/solution.py
+++ b/solution.py
@@ -136,7 +136,6 @@
     tables = (whole, whole, two_chunks(helped, length - helped), two_chunks(0, helped))
     heads = width // HD
     full = PEERS * width
-    tile = min(256, width)
     section = lax.axis_index("section")
     rank = lax.axis_index("tp")
     x = rank % RING
@@ -232,31 +231,15 @@
     def consume_cot(blocks, first=False):
         for block in blocks:
             base = pl.multiple_of(block * width, width)
-
-            @pl.loop(0, width // tile)
-            def _(n):
-                at_n = pl.multiple_of(n * tile, tile)
-                term = dot(cots[block], wo[pl.ds(at_n, tile), pl.ds(base, width)], NT)
-                if first:
-                    acc[:, pl.ds(at_n, tile)] = term
-                else:
-                    acc[:, pl.ds(at_n, tile)] += term
-
+            term = dot(cots[block], wo[:, pl.ds(base, width)], NT)
+            acc[...] = term if first else acc[...] + term
             first = False
 
     def consume_rows(buf, blocks, first=False):
         for block in blocks:
             base = pl.multiple_of(block * width, width)
-
-            @pl.loop(0, width // tile)
-            def _(n):
-                at_n = pl.multiple_of(n * tile, tile)
-                term = dot(buf[block], wv[pl.ds(base, width), pl.ds(at_n, tile)], NN)
-                if first:
-                    acc[:, pl.ds(at_n, tile)] = term
-                else:
-                    acc[:, pl.ds(at_n, tile)] += term
-
+            term = dot(buf[block], wv[pl.ds(base, width), :], NN)
+            acc[...] = term if first else acc[...] + term
             first = False
 
     blocks = [at(*rel) for rel in BLOCKS]
@@ -352,26 +335,15 @@
     def grad_term(rel):
         block = at(*rel)
         base = pl.multiple_of(block * width, width)
-
-        @pl.loop(0, width // tile)
-        def _(n):
-            at_n = pl.multiple_of(n * tile, tile)
-            row_n = pl.multiple_of(base + at_n, tile)
-            term = dot(grad_val[...], wv[pl.ds(row_n, tile), :], NT)
-            if rel == OWNER:
-                term = term + grad_q[:, pl.ds(at_n, tile)]
-            part_g[block, :, pl.ds(at_n, tile)] = term.astype(BF16)
+        term = dot(grad_val[...], wv[pl.ds(base, width), :], NT)
+        if rel == OWNER:
+            term = term + grad_q[...]
+        part_g[block] = term.astype(BF16)
 
     def head_term(rel):
         block = at(*rel)
         base = pl.multiple_of(block * width, width)
-
-        @pl.loop(0, width // tile)
-        def _(n):
-            at_n = pl.multiple_of(n * tile, tile)
-            col_n = pl.multiple_of(base + at_n, tile)
-            term = dot(ctx[...], wo[:, pl.ds(col_n, tile)], NN)
-            part_h[block, :, pl.ds(at_n, tile)] = term.astype(BF16)
+        part_h[block] = dot(ctx[...], wo[:, pl.ds(base, width)], NN).astype(BF16)
 
     gain = gain_ref[:, pl.ds(pl.multiple_of(rank * width, width), width)]
     top, bottom = pl.ds(0, helped), pl.ds(helped, length - helped)
@@ -495,9 +467,8 @@
     consume_cot(near, first=True)
     gather_relay(cots, 0, 2)
 
-    @pl.loop(0, heads)
-    def _(head):
-        cols = pl.ds(pl.multiple_of(head * HD, HD), HD)
+    for head in range(heads):
+        cols = pl.ds(head * HD, HD)
         v = val_f[:, cols]
         low = probabilities(rows_f[me, :, cols], v).astype(BF16)
         ctx[:, cols] = dot(low, v, NN).astype(BF16)
@@ -531,9 +502,8 @@
         val_b[...] = val_f[...]
         query[...] = rows_f[me]
 
-    @pl.loop(0, heads)
-    def _(head):
-        cols = pl.ds(pl.multiple_of(head * HD, HD), HD)
+    for head in range(heads):
+        cols = pl.ds(head * HD, HD)
         q = query[:, cols]
         v = val_b[:, cols]
         g = grad_ctx[:, cols]

time: 133 us -> 124 us (0.932)
  Pallas kernels: 132 us -> 123 us
    pallas_call x1, Pallas kernels: 130 us -> 121 us  [body(): pl.pallas_call(functools.partial(kernel, sections), out_shape=out_shape,...]
where the time goes in v4:
time: 124 us
  Pallas kernels  123 us (99%)
    pallas_call x1, Pallas kernels, body(): pl.pallas_call(functools.partial(kernel, sections), out_shape=out_shape,...  121 us

profile of v4, /device:TPU:96, one launch (start us, length us, event | category | flops | bytes accessed | tf_op | source)
XLA Modules:
  0.0 123.7 jit_solution(16484088518253998802)
XLA Ops:
  0.6 120.8 %shard_map.102 = (bf16[256,768]{1,0:T(8,128)(2,1)}, bf16[256,768]{1,0:T(8,128)(2,1)}, bf16[256,768]{1,0:T(8,128)(2,1)}, f32[1,768]{1,0:T(1,128)}) custom-call(bf16[256,768]{1,0:T(8,128)(2,1)} %bitcast.11, bf16[256,768]{1,0:T(8,128)(2,1)} %bitcast.12, bf16[2,256,768]{2,1,0:T(8,128)(2,1)} %bitcast.10, s32[16]{0:T(128)} %slot_ref.1, f32[1,6144]{1,0:T(1,128)} %gain_ref.1, ...), custom_call_target="tpu_custom_call" | custom-call | tf_op jit(solution)/shard_map/pallas_call | solution.py:629
  121.4 2.1 %shard_map.103 = (bf16[256,768]{1,0:T(8,128)(2,1)}, bf16[256,768]{1,0:T(8,128)(2,1)}, bf16[256,768]{1,0:T(8,128)(2,1)}, f32[1,768]{1,0:T(1,128)}) custom-call(bf16[256,768]{1,0:T(8,128)(2,1)} %get-tuple-element.12.refs_0_, bf16[256,768]{1,0:T(8,128)(2,1)} %get-tuple-element.13.refs_1_, bf16[256,768]{1,0:T(8,128)(2,1)} %get-tuple-element.14.refs_2_, ...), custom_call_target="tpu_custom_call" | custom-call | tf_op jit(solution)/shard_map/pallas_call | solution.py:681

commit v5 on v4

--- a/solution.py
+++ b/solution.py
@@ -130,7 +130,7 @@
 ):
     length, width = arr.shape
     half = length // 2
-    helped = half
+    helped = length * 3 // 8
     chunks = two_chunks(0, length)
     whole = three_chunks(length)
     tables = (whole, whole, two_chunks(helped, length - helped), two_chunks(0, helped))
@@ -652,7 +652,7 @@
             pltpu.VMEM((2, length, width), BF16),
             share,
             share,
-            pltpu.VMEM((PEERS, length // 2, width), BF16),
+            pltpu.VMEM((PEERS, length * 3 // 8, width), BF16),
             share,
             wide,
             pltpu.VMEM((length, HD), F32),

time: 124 us -> 123 us (level); the launches traced: 124 us -> 121 us
  Pallas kernels: 123 us -> 120 us
    pallas_call x1, Pallas kernels: 121 us -> 118 us  [body(): pl.pallas_call(functools.partial(kernel, sections), out_shape=out_shape,...]
where the time goes in v5:
time: 123 us; the launch traced here: 121 us
  Pallas kernels  120 us (98%)
    pallas_call x1, Pallas kernels, body(): pl.pallas_call(functools.partial(kernel, sections), out_shape=out_shape,...  118 us

profile of v5, /device:TPU:96, one launch (start us, length us, event | category | flops | bytes accessed | tf_op | source)
XLA Modules:
  0.0 121.2 jit_solution(14511480769320887087)
XLA Ops:
  0.6 118.3 %shard_map.102 = (bf16[256,768]{1,0:T(8,128)(2,1)}, bf16[256,768]{1,0:T(8,128)(2,1)}, bf16[256,768]{1,0:T(8,128)(2,1)}, f32[1,768]{1,0:T(1,128)}) custom-call(bf16[256,768]{1,0:T(8,128)(2,1)} %bitcast.11, bf16[256,768]{1,0:T(8,128)(2,1)} %bitcast.12, bf16[2,256,768]{2,1,0:T(8,128)(2,1)} %bitcast.10, s32[16]{0:T(128)} %slot_ref.1, f32[1,6144]{1,0:T(1,128)} %gain_ref.1, ...), custom_call_target="tpu_custom_call" | custom-call | tf_op jit(solution)/shard_map/pallas_call | solution.py:629
  118.9 2.1 %shard_map.103 = (bf16[256,768]{1,0:T(8,128)(2,1)}, bf16[256,768]{1,0:T(8,128)(2,1)}, bf16[256,768]{1,0:T(8,128)(2,1)}, f32[1,768]{1,0:T(1,128)}) custom-call(bf16[256,768]{1,0:T(8,128)(2,1)} %get-tuple-element.12.refs_0_, bf16[256,768]{1,0:T(8,128)(2,1)} %get-tuple-element.13.refs_1_, bf16[256,768]{1,0:T(8,128)(2,1)} %get-tuple-element.14.refs_2_, ...), custom_call_target="tpu_custom_call" | custom-call | tf_op jit(solution)/shard_map/pallas_call | solution.py:681
